TPU v7x, 32 devices: a whole 2x2x4 slice. The times are simulated.
32 devices in a mesh: gx: 8 (over z, x), gy: 4 (over y, core).
Axes of the slice: x: 2, y: 2, z: 4, core: 2. Of those that a mesh axis runs over, the one named last changes fastest.
Arguments:
- states: bfloat16 [2, 64, 8, 64, 512], P(None, None, None, 'gx', 'gy'), may hold values from -6 to 6, as said below
- class_map: int32 [8, 64, 512], P(None, 'gx', 'gy'), may hold values from 0 to 7
- perm_table: float32 [8], replicated, may hold values from 0.05 to 1
- candidates: int32 [8, 4, 64], replicated, may hold values from 0 to 8191, as said below
- merge_order: int32 [31, 128], replicated, may hold values from 0 to 127, each once within a row
Outputs:
- flux: bfloat16 [64, 8, 64, 512], P(None, None, 'gx', 'gy')
- kept_rows: float32 [31, 64, 64], replicated
Inputs may be any that keep to these rules, and one draw needn't show every extreme that they name: states[0] is pressure; states[1] is water saturation, between 0.05 and 0.95. `candidates`: each tile's 64 entries are distinct cell numbers (z * 8 + x) * 128 + y of that tile's own cells. `merge_order`: each row is a permutation of 0 to 127.
All inputs are finite; a program needn't handle non-finite values.
Results may differ from a plain program's by a relative error of at most 0.001.
Values may be sent and summed in bfloat16 or wider, within the bound.
A program may use at most 128 MiB of HBM per device.

v0:
```python
import jax
import jax.numpy as jnp
from jax import lax
from jax.sharding import PartitionSpec as P


def padded_2(block, sides, width):
    for axis, dim in sides:
        count = lax.axis_size(axis)
        forward = [(i, i + 1) for i in range(count - 1)]
        forward.append((count - 1, 0))
        backward = [(target, source) for source, target in forward]
        low = lax.ppermute(
            lax.slice_in_dim(block, block.shape[dim] - width, None, axis=dim), axis, forward
        )
        high = lax.ppermute(lax.slice_in_dim(block, 0, width, axis=dim), axis, backward)
        block = jnp.concatenate([low, block, high], axis=dim)
    return block


def face_term(p_here, m_here, k_here, p_next, m_next, k_next):
    transmit = 2.0 * k_here * k_next / (k_here + k_next)
    return transmit * (0.5 * (m_here + m_next)) * (p_next - p_here)


def kept_sources(tile_count, kept_count, merge_order):
    level_ids = jnp.arange(tile_count * kept_count, dtype=jnp.int32).reshape(tile_count, kept_count)
    offset = 0
    kept_list = []
    for level_num in range(tile_count.bit_length() - 1):
        groups = level_ids.shape[0] // 2
        paired = level_ids.reshape(groups, 2 * kept_count)
        node_order = merge_order[offset : offset + groups, :kept_count]
        level_ids = jnp.take_along_axis(paired, node_order, axis=1)
        kept_list.append(level_ids)
        offset = offset + groups
    return jnp.concatenate(kept_list, axis=0)


def neighbour(centre, padded, which):
    if which == 0:
        return centre
    if which in (1, 2):
        row = lax.broadcasted_iota(jnp.int32, centre.shape, centre.ndim - 2)
        height = centre.shape[-2]
        if which == 1:
            return jnp.where(row == height - 1, padded[..., -1:, 1:-1], jnp.roll(centre, -1, -2))
        return jnp.where(row == 0, padded[..., :1, 1:-1], jnp.roll(centre, 1, -2))
    if which in (3, 4):
        column = lax.broadcasted_iota(jnp.int32, centre.shape, centre.ndim - 1)
        width_y = centre.shape[-1]
        if which == 3:
            return jnp.where(
                column == width_y - 1, padded[..., 1:-1, -1:], jnp.roll(centre, -1, -1)
            )
        return jnp.where(column == 0, padded[..., 1:-1, :1], jnp.roll(centre, 1, -1))
    zero_plane = jnp.zeros(centre.shape[:-3] + (1,) + centre.shape[-2:], centre.dtype)
    if which == 5:
        return jnp.concatenate([centre[..., 1:, :, :], zero_plane], axis=-3)
    return jnp.concatenate([zero_plane, centre[..., :-1, :, :]], axis=-3)


def full_flux(states, padded, perm_here, perm_pad):

    def fields(which):
        pressure = neighbour(states[0], padded[0], which).astype(jnp.float32)
        saturation = neighbour(states[1], padded[1], which).astype(jnp.float32)
        return (pressure, saturation * saturation, neighbour(perm_here, perm_pad, which)[None])

    here_p, here_m, here_k = fields(0)

    def side(which):
        there_p, there_m, there_k = fields(which)
        return face_term(here_p, here_m, here_k, there_p, there_m, there_k)

    summed = side(1) + side(2)
    summed = summed + side(3)
    summed = summed + side(4)
    summed = summed + side(5)
    summed = summed + side(6)
    return summed


def collect(my_rows, merge_order):
    kept_count = my_rows.shape[0]
    tile_count = lax.axis_size("gx") * lax.axis_size("gy")
    kept_ids = kept_sources(tile_count, kept_count, merge_order)
    column = lax.all_gather(my_rows[None, None], "gy", axis=1, tiled=True)
    gathered = lax.all_gather(column, "gx", axis=0, tiled=True)
    flat_rows = gathered.reshape(tile_count * kept_count, my_rows.shape[1])
    return flat_rows[kept_ids.reshape(-1)].reshape(kept_ids.shape + (my_rows.shape[1],))


def local(states, class_map, perm_table, candidates, merge_order):
    padded = padded_2(states, (("gx", 3), ("gy", 4)), 1)
    class_pad = padded_2(class_map, (("gx", 1), ("gy", 2)), 1)
    perm_pad = jnp.zeros(class_pad.shape, jnp.float32)
    perm_here = jnp.zeros(class_map.shape, jnp.float32)
    for class_num in range(perm_table.shape[0]):
        perm_pad = perm_pad + jnp.where(class_pad == class_num, perm_table[class_num], 0.0)
        perm_here = perm_here + jnp.where(class_map == class_num, perm_table[class_num], 0.0)
    tile_x = lax.axis_index("gx")
    tile_y = lax.axis_index("gy")
    tile_cells = lax.dynamic_index_in_dim(
        lax.dynamic_index_in_dim(candidates, tile_x, 0, False), tile_y, 0, False
    )
    cell_total = class_map.shape[0] * class_map.shape[1] * class_map.shape[2]
    cell_ids = lax.broadcasted_iota(jnp.int32, (cell_total, tile_cells.shape[0]), 0)
    picker = jnp.where(cell_ids == tile_cells[None, :], 1.0, 0.0).astype(jnp.float32)
    flux_full = full_flux(states, padded, perm_here, perm_pad)
    flat_flux = flux_full.reshape(flux_full.shape[0], -1)
    my_rows = jnp.einsum(
        "sc,ci->is",
        flat_flux,
        picker,
        precision=lax.Precision.HIGHEST,
        preferred_element_type=jnp.float32,
    )
    kept_rows = collect(my_rows, merge_order)
    return (flux_full.astype(jnp.bfloat16), kept_rows)


def solution(mesh):
    in_specs = (P(None, None, None, "gx", "gy"), P(None, "gx", "gy"), P(), P(), P())
    out_specs = (P(None, None, "gx", "gy"), P())
    return jax.shard_map(local, mesh=mesh, in_specs=in_specs, out_specs=out_specs, check_vma=False)
```

profile of v0, /device:TPU:0, one launch (start us, length us, event | category | flops | bytes accessed | tf_op | source)
XLA Modules:
  0.0 185.5 jit_solution(5166065720969816784)
XLA Ops:
  1.5 3.0 %collective-permute-start.4 = (s32[8,1,128]{2,0,1:T(8,128)S(1)}, s32[8,1,128]{2,0,1:T(8,128)S(1)}, u32[]{:S(2)}, u32[]{:S(2)}) collective-permute-start(s32[8,1,128]{2,0,1:T(8,128)S(1)} %copy.79), channel_id=1, source_target_pairs={{0,4},{4,8},{8,12},{12,16},{16,20},{20,24},{24,28},{28,0},{1,5},{5... | collective-permute-start | bytes 12296 | tf_op jit(solution)/shard_map/ppermute | solution.py:13
  4.5 3.1 %collective-permute-start.5 = (s32[8,1,128]{2,0,1:T(8,128)S(1)}, s32[8,1,128]{2,0,1:T(8,128)S(1)}, u32[]{:S(2)}, u32[]{:S(2)}) collective-permute-start(s32[8,1,128]{2,0,1:T(8,128)S(1)} %copy.80), channel_id=1, source_target_pairs={{4,0},{8,4},{12,8},{16,12},{20,16},{24,20},{28,24},{0,28},{5,1},{9... | collective-permute-start | bytes 12296 | tf_op jit(solution)/shard_map/ppermute | solution.py:16
  7.6 3.2 %fusion.30 = (bf16[2,64,8,1,128]{4,3,2,1,0:T(2,128)(2,1)S(1)}, bf16[2,64,8,1,128]{4,3,2,1,0:T(2,128)(2,1)S(1)}) fusion(bf16[2,64,8,8,128]{4,3,2,1,0:T(8,128)(2,1)} %param.5), kind=kLoop, calls=%fused_computation.105 | loop fusion | bytes 1048576 | tf_op jit(solution)/shard_map/slice | solution.py:16
  12.3 4.7 %collective-permute-start.1 = (bf16[2,64,8,1,128]{4,2,1,3,0:T(8,128)(2,1)}, bf16[2,64,8,1,128]{4,2,1,3,0:T(8,128)(2,1)}, u32[]{:S(2)}, u32[]{:S(2)}) collective-permute-start(bf16[2,64,8,1,128]{4,2,1,3,0:T(8,128)(2,1)} %copy.82), channel_id=1, source_target_pairs={{4,0},{8,4},{12,8},{16,12},{20,16},{24,20},{28,24},{0,28},{5,1},{9... | collective-permute-start | bytes 786440 | tf_op jit(solution)/shard_map/ppermute | solution.py:16
  17.7 5.0 %select_add_fusion.1 = f32[8,8,128]{2,1,0:T(8,128)S(1)} fusion(s32[8,8,128]{2,1,0:T(8,128)S(1)} %copy-done.3, f32[]{:T(128)} %bitcast.10, f32[]{:T(128)} %bitcast.9, f32[]{:T(128)} %bitcast.8, f32[]{:T(128)} %bitcast.7, f32[]{:T(128)} %bitcast.6, f32[]{:T(128)} %bitcast.5, f32[]{:T(128)} %bitcast.4, f32[]{:T(128)} %bitcast.3), kind=kLoop, calls=%fused_computation.67 | loop fusion | flops 188416 | bytes 65568 | tf_op jit(solution)/shard_map/add | solution.py:101
  38.1 6.8 %gather_fusion.2 = s32[1024]{0:T(1024)S(1)} fusion(s32[16,128]{1,0:T(8,128)S(1)} %multiply_add_fusion, s32[1024]{0:T(1024)S(1)} %reshape.191), kind=kCustom, calls=%fused_computation.2 | custom fusion | bytes 16384 | tf_op jit(solution)/shard_map/jit(take_along_axis)/gather | solution.py:34
  57.3 5.1 %select_add_fusion = f32[8,10,130]{2,0,1:T(8,128)S(1)} fusion(s32[8,10,1]{2,0,1:T(8,128)S(1)} %collective-permute-done.7, s32[8,10,128]{2,0,1:T(8,128)S(1)} %constant_dynamic-update-slice_fusion.3, s32[8,10,1]{2,0,1:T(8,128)S(1)} %collective-permute-done.6, f32[]{:T(128)} %bitcast.10, f32[]{:T(128)} %bitcast.9, f32[]{:T(128)} %bitcast.8, f32[]{:T(128)} %bitcast.7, ...), kind=kLoop, calls=%fused_computation.49 | loop fusion | flops 260000 | bytes 83232 | tf_op jit(solution)/shard_map/add | solution.py:100
  68.1 3.4 %fusion.29 = (bf16[2,64,8,10,1]{4,2,1,3,0:T(8,128)(2,1)}, bf16[2,64,8,10,1]{4,2,1,3,0:T(8,128)(2,1)}) fusion(bf16[2,64,8,10,128]{4,2,1,3,0:T(8,128)(2,1)S(1)} %constant_dynamic-update-slice_fusion), kind=kLoop, calls=%fused_computation.104 | loop fusion | bytes 81920 | tf_op jit(solution)/shard_map/slice | solution.py:14
  71.5 3.7 %copy.51 = bf16[2,64,8,10,1]{1,2,4,3,0:T(8,128)(2,1)} copy(bf16[2,64,8,10,1]{4,2,1,3,0:T(8,128)(2,1)} %get-tuple-element.14) | data formatting | bytes 40960 | tf_op jit(solution)/shard_map/slice | solution.py:14
  76.9 3.7 %copy.52 = bf16[2,64,8,10,1]{1,2,4,3,0:T(8,128)(2,1)} copy(bf16[2,64,8,10,1]{4,2,1,3,0:T(8,128)(2,1)} %get-tuple-element.15) | data formatting | bytes 40960 | tf_op jit(solution)/shard_map/slice | solution.py:16
  80.7 6.7 %divide_multiply_fusion.3 = (f32[8,8,128]{2,1,0:T(8,128)S(1)}, f32[8,8,128]{2,1,0:T(8,128)S(1)}, f32[8,8,128]{2,1,0:T(8,128)}, f32[8,8,128]{2,1,0:T(8,128)}, f32[8,8,128]{2,1,0:T(8,128)}, /*index=5*/f32[8,8,128]{2,1,0:T(8,128)}) fusion(f32[8,1,128]{2,1,0:T(1,128)S(1)} %copy-done.7, f32[8,7,128]{2,1,0:T(8,128)} %get-tuple-element.52, ...), kind=kLoop, calls=%fused_computation.66 | loop fusion | flops 458752 | bytes 426800 | tf_op jit(solution)/shard_map/mul | solution.py:23
  87.3 3.1 %copy.53 = bf16[2,64,8,10,1]{4,2,1,3,0:T(8,128)(2,1)} copy(bf16[2,64,8,10,1]{1,2,4,3,0:T(8,128)(2,1)} %collective-permute-done.2) | data formatting | bytes 40960 | tf_op jit(solution)/shard_map/ppermute | solution.py:13
  90.5 3.2 %copy.54 = bf16[2,64,8,10,1]{4,2,1,3,0:T(8,128)(2,1)} copy(bf16[2,64,8,10,1]{1,2,4,3,0:T(8,128)(2,1)} %collective-permute-done.3) | data formatting | bytes 40960 | tf_op jit(solution)/shard_map/ppermute | solution.py:16
  93.6 6.1 %pad_maximum_fusion = bf16[2,64,8,10,130]{4,2,1,3,0:T(8,128)(2,1)S(1)} fusion(bf16[2,64,8,10,1]{4,2,1,3,0:T(8,128)(2,1)} %copy.54, bf16[2,64,8,10,128]{4,2,1,3,0:T(8,128)(2,1)} %copy-done.2, bf16[2,64,8,10,1]{4,2,1,3,0:T(8,128)(2,1)} %copy.53), kind=kLoop, calls=%fused_computation.6 | loop fusion | flops 7987200 | bytes 5324800 | tf_op jit(solution)/shard_map/concatenate | solution.py:17
  101.3 2.8 %fusion.27 = (bf16[64,8,8,1]{3,1,0,2:T(8,128)(2,1)}, bf16[64,8,8,1]{3,1,0,2:T(8,128)(2,1)}, bf16[64,8,8,1]{3,1,0,2:T(8,128)(2,1)}, bf16[64,8,8,1]{3,1,0,2:T(8,128)(2,1)}) fusion(bf16[64,8,10,130]{3,1,0,2:T(8,128)(2,1)S(1)} %get-tuple-element.4, bf16[64,8,10,130]{3,1,0,2:T(8,128)(2,1)S(1)} %get-tuple-element.5), kind=kLoop, calls=%fused_computation.102 | loop fusion | bytes 65536 | tf_op jit(solution)/shard_map/slice | solution.py:54
  104.1 4.9 %copy.68 = bf16[64,8,8,1]{2,1,0,3:T(8,128)(2,1)} copy(bf16[64,8,8,1]{3,1,0,2:T(8,128)(2,1)} %get-tuple-element.10) | data formatting | bytes 16384 | tf_op jit(solution)/shard_map/jit(_where)/broadcast_in_dim | solution.py:53
  109.0 5.0 %copy.69 = bf16[64,8,8,1]{2,1,0,3:T(8,128)(2,1)} copy(bf16[64,8,8,1]{3,1,0,2:T(8,128)(2,1)} %get-tuple-element.89) | data formatting | bytes 16384 | tf_op jit(solution)/shard_map/jit(_where)/broadcast_in_dim | solution.py:53
  114.0 4.9 %copy.70 = bf16[64,8,8,1]{2,1,0,3:T(8,128)(2,1)} copy(bf16[64,8,8,1]{3,1,0,2:T(8,128)(2,1)} %get-tuple-element.11) | data formatting | bytes 16384 | tf_op jit(solution)/shard_map/jit(_where)/broadcast_in_dim | solution.py:56
  118.9 5.2 %copy.71 = bf16[64,8,8,1]{2,1,0,3:T(8,128)(2,1)} copy(bf16[64,8,8,1]{3,1,0,2:T(8,128)(2,1)} %get-tuple-element.88) | data formatting | bytes 16384 | tf_op jit(solution)/shard_map/jit(_where)/broadcast_in_dim | solution.py:56
  124.1 12.4 %fusion.25 = (bf16[64,8,8,128]{3,2,1,0:T(8,128)(2,1)}, f32[64,8,8,128]{3,2,1,0:T(8,128)S(1)}) fusion(bf16[64,7,8,128]{3,2,1,0:T(8,128)(2,1)} %get-tuple-element.80, f32[8,8,128]{2,1,0:T(8,128)} %get-tuple-element.51, bf16[64,7,8,128]{3,2,1,0:T(8,128)(2,1)} %get-tuple-element.37, bf16[64,7,8,128]{3,2,1,0:T(8,128)(2,1)} %get-tuple-element.81, ...), kind=kLoop, calls=%fused_computation.101 | loop fusion | flops 47710208 | bytes 18055440 | tf_op jit(solution)/shard_map/convert_element_type | solution.py:120
  136.6 2.9 %fusion.11 = f32[64,64]{1,0:T(8,128)S(1)} fusion(f32[8,8,64,128]{3,2,1,0:T(8,128)S(1)} %bitcast.76, s32[64]{0:T(128)S(1)} %copy-done.15), kind=kOutput, calls=%fused_computation.26 | convolution fusion | flops 403701760 | bytes 2113792 | tf_op jit(solution)/shard_map/sc,ci->is/dot_general | solution.py:112
  139.5 5.4 %all-gather = f32[256,64]{1,0:T(8,128)S(1)} all-gather(f32[64,64]{1,0:T(8,128)S(1)} %fusion.11), channel_id=2, replica_groups=mesh['gx'=8,'gy'=4] {'gy'}, dimensions={0}, use_global_device_ids=true | all-gather | bytes 81920 | tf_op jit(solution)/shard_map/all_gather | solution.py:88
  144.9 33.0 %all_gather.7 = f32[8,4,64,64]{3,2,1,0:T(8,128)S(1)} all-gather(f32[1,4,64,64]{3,2,1,0:T(8,128)S(1)} %bitcast.82), channel_id=1, replica_groups=mesh['gx'=8,'gy'=4] {'gx'}, dimensions={0}, use_global_device_ids=true | all-gather | bytes 589824 | tf_op jit(solution)/shard_map/all_gather | solution.py:89
  177.9 7.6 %gather_fusion.1 = f32[1984,64]{1,0:T(8,128)} fusion(f32[2048,64]{1,0:T(8,128)S(1)} %bitcast.75, s32[2048]{0:T(1024)S(1)} %pad_clamp_fusion), kind=kCustom, calls=%fused_computation.1 | custom fusion | bytes 1023744 | tf_op jit(solution)/shard_map/gather | solution.py:91
  (110 shorter events, 39.5 us)
Async XLA Ops:
  0.6 55.0 %copy-start = (s32[8,4,64]{2,1,0:T(4,128)S(1)}, s32[8,4,64]{2,1,0:T(4,128)}, u32[]{:S(2)}) copy-start(s32[8,4,64]{2,1,0:T(4,128)} %param.8) | copy-start | bytes 24580
  0.6 17.1 %copy-start.3 = (s32[8,8,128]{2,1,0:T(8,128)S(1)}, s32[8,8,128]{2,1,0:T(8,128)}, u32[]{:S(2)}) copy-start(s32[8,8,128]{2,1,0:T(8,128)} %param.6) | copy-start | bytes 98308
  0.7 16.4 %copy-start.6 = (f32[8]{0:T(128)S(1)}, f32[8]{0:T(128)}, u32[]{:S(2)}) copy-start(f32[8]{0:T(128)} %param.7) | copy-start | bytes 100
  1.5 52.2 %collective-permute-start.4 = (s32[8,1,128]{2,0,1:T(8,128)S(1)}, s32[8,1,128]{2,0,1:T(8,128)S(1)}, u32[]{:S(2)}, u32[]{:S(2)}) collective-permute-start(s32[8,1,128]{2,0,1:T(8,128)S(1)} %copy.79), channel_id=1, source_target_pairs={{0,4},{4,8},{8,12},{12,16},{16,20},{20,24},{24,28},{28,0},{1,5},{5... | collective-permute-start | bytes 12296 | tf_op jit(solution)/shard_map/ppermute | solution.py:13
  4.5 22.1 %copy-start.1 = (bf16[2,64,8,8,128]{4,3,2,1,0:T(8,128)(2,1)S(1)}, bf16[2,64,8,8,128]{4,3,2,1,0:T(8,128)(2,1)}, u32[]{:S(2)}) copy-start(bf16[2,64,8,8,128]{4,3,2,1,0:T(8,128)(2,1)} %param.5) | copy-start | bytes 6291460
  4.5 49.2 %collective-permute-start.5 = (s32[8,1,128]{2,0,1:T(8,128)S(1)}, s32[8,1,128]{2,0,1:T(8,128)S(1)}, u32[]{:S(2)}, u32[]{:S(2)}) collective-permute-start(s32[8,1,128]{2,0,1:T(8,128)S(1)} %copy.80), channel_id=1, source_target_pairs={{4,0},{8,4},{12,8},{16,12},{20,16},{24,20},{28,24},{0,28},{5,1},{9... | collective-permute-start | bytes 12296 | tf_op jit(solution)/shard_map/ppermute | solution.py:16
  11.6 54.0 %collective-permute-start = (bf16[2,64,8,1,128]{4,2,1,3,0:T(8,128)(2,1)}, bf16[2,64,8,1,128]{4,2,1,3,0:T(8,128)(2,1)}, u32[]{:S(2)}, u32[]{:S(2)}) collective-permute-start(bf16[2,64,8,1,128]{4,2,1,3,0:T(8,128)(2,1)} %copy.81), channel_id=1, source_target_pairs={{0,4},{4,8},{8,12},{12,16},{16,20},{20,24},{24,28},{28,0},{1,5},{5... | collective-permute-start | bytes 786440 | tf_op jit(solution)/shard_map/ppermute | solution.py:13
  12.3 54.8 %collective-permute-start.1 = (bf16[2,64,8,1,128]{4,2,1,3,0:T(8,128)(2,1)}, bf16[2,64,8,1,128]{4,2,1,3,0:T(8,128)(2,1)}, u32[]{:S(2)}, u32[]{:S(2)}) collective-permute-start(bf16[2,64,8,1,128]{4,2,1,3,0:T(8,128)(2,1)} %copy.82), channel_id=1, source_target_pairs={{4,0},{8,4},{12,8},{16,12},{20,16},{24,20},{28,24},{0,28},{5,1},{9... | collective-permute-start | bytes 786440 | tf_op jit(solution)/shard_map/ppermute | solution.py:16
  36.4 1.6 copy-start.5
  53.9 3.4 %collective-permute-start.6 = (s32[8,10,1]{2,0,1:T(8,128)S(1)}, s32[8,10,1]{2,0,1:T(8,128)S(1)}, u32[]{:S(2)}, u32[]{:S(2)}) collective-permute-start(s32[8,10,1]{2,0,1:T(8,128)S(1)} %get-tuple-element.44), channel_id=1, source_target_pairs={{0,1},{1,2},{2,3},{3,0},{4,5},{5,6},{6,7},{7,4},{8,9},{9,10},{10,1... | collective-permute-start | bytes 968 | tf_op jit(solution)/shard_map/ppermute | solution.py:13
  53.9 3.4 %collective-permute-start.7 = (s32[8,10,1]{2,0,1:T(8,128)S(1)}, s32[8,10,1]{2,0,1:T(8,128)S(1)}, u32[]{:S(2)}, u32[]{:S(2)}) collective-permute-start(s32[8,10,1]{2,0,1:T(8,128)S(1)} %get-tuple-element.45), channel_id=1, source_target_pairs={{1,0},{2,1},{3,2},{0,3},{5,4},{6,5},{7,6},{4,7},{9,8},{10,9},{11,1... | collective-permute-start | bytes 968 | tf_op jit(solution)/shard_map/ppermute | solution.py:16
  68.1 3.4 %copy-start.2 = (bf16[2,64,8,10,128]{4,2,1,3,0:T(8,128)(2,1)}, bf16[2,64,8,10,128]{4,2,1,3,0:T(8,128)(2,1)S(1)}, u32[]{:S(2)}) copy-start(bf16[2,64,8,10,128]{4,2,1,3,0:T(8,128)(2,1)S(1)} %constant_dynamic-update-slice_fusion) | copy-start | bytes 7864324
  71.5 9.1 %copy-start.7 = (f32[8,1,128]{2,1,0:T(1,128)S(1)}, f32[8,1,128]{2,1,0:T(1,128)}, u32[]{:S(2)}) copy-start(f32[8,1,128]{2,1,0:T(1,128)} %get-tuple-element.54) | copy-start | bytes 12292
  71.5 9.1 %copy-start.8 = (f32[8,1,128]{2,1,0:T(1,128)S(1)}, f32[8,1,128]{2,1,0:T(1,128)}, u32[]{:S(2)}) copy-start(f32[8,1,128]{2,1,0:T(1,128)} %get-tuple-element.55) | copy-start | bytes 12292
  71.5 9.1 %copy-start.9 = (f32[8,128]{1,0:T(8,128)S(1)}, f32[8,128]{1,0:T(8,128)}, u32[]{:S(2)}) copy-start(f32[8,128]{1,0:T(8,128)} %get-tuple-element.40) | copy-start | bytes 12292
  71.5 9.1 %copy-start.10 = (f32[8,128]{1,0:T(8,128)S(1)}, f32[8,128]{1,0:T(8,128)}, u32[]{:S(2)}) copy-start(f32[8,128]{1,0:T(8,128)} %get-tuple-element.41) | copy-start | bytes 12292
  75.2 12.1 %collective-permute-start.2 = (bf16[2,64,8,10,1]{1,2,4,3,0:T(8,128)(2,1)}, bf16[2,64,8,10,1]{1,2,4,3,0:T(8,128)(2,1)}, u32[]{:S(2)}, u32[]{:S(2)}) collective-permute-start(bf16[2,64,8,10,1]{1,2,4,3,0:T(8,128)(2,1)} %copy.51), channel_id=1, source_target_pairs={{0,1},{1,2},{2,3},{3,0},{4,5},{5,6},{6,7},{7,4},{8,9},{9,10},{10,1... | collective-permute-start | bytes 61448 | tf_op jit(solution)/shard_map/ppermute | solution.py:13
  80.6 9.9 %collective-permute-start.3 = (bf16[2,64,8,10,1]{1,2,4,3,0:T(8,128)(2,1)}, bf16[2,64,8,10,1]{1,2,4,3,0:T(8,128)(2,1)}, u32[]{:S(2)}, u32[]{:S(2)}) collective-permute-start(bf16[2,64,8,10,1]{1,2,4,3,0:T(8,128)(2,1)} %copy.52), channel_id=1, source_target_pairs={{1,0},{2,1},{3,2},{0,3},{5,4},{6,5},{7,6},{4,7},{9,8},{10,9},{11,1... | collective-permute-start | bytes 61448 | tf_op jit(solution)/shard_map/ppermute | solution.py:16
  109.0 15.1 %copy-start.4 = (f32[8,8,128]{2,1,0:T(8,128)S(1)}, f32[8,8,128]{2,1,0:T(8,128)}, u32[]{:S(2)}) copy-start(f32[8,8,128]{2,1,0:T(8,128)} %get-tuple-element.48) | copy-start | bytes 98308
  109.0 15.1 %copy-start.11 = (pred[128]{0:T(512)(128)(4,1)S(1)}, pred[128]{0:T(512)(128)(4,1)}, u32[]{:S(2)}) copy-start(pred[128]{0:T(512)(128)(4,1)} %get-tuple-element.82) | copy-start | bytes 388
  109.0 15.1 %copy-start.12 = (pred[128]{0:T(512)(128)(4,1)S(1)}, pred[128]{0:T(512)(128)(4,1)}, u32[]{:S(2)}) copy-start(pred[128]{0:T(512)(128)(4,1)} %get-tuple-element.83) | copy-start | bytes 388
  109.0 15.1 %copy-start.13 = (pred[8]{0:T(512)(128)(4,1)S(1)}, pred[8]{0:T(512)(128)(4,1)}, u32[]{:S(2)}) copy-start(pred[8]{0:T(512)(128)(4,1)} %get-tuple-element.84) | copy-start | bytes 28
  109.0 15.1 %copy-start.14 = (pred[8]{0:T(512)(128)(4,1)S(1)}, pred[8]{0:T(512)(128)(4,1)}, u32[]{:S(2)}) copy-start(pred[8]{0:T(512)(128)(4,1)} %get-tuple-element.85) | copy-start | bytes 28
  124.1 12.4 %copy-start.15 = (s32[64]{0:T(128)S(1)}, s32[64]{0:T(128)}, u32[]{:S(2)}) copy-start(s32[64]{0:T(128)} %dynamic-slice_bitcast_fusion) | copy-start | bytes 772
where the time goes:
time: 187 us; the launch traced here: 186 us
  local copies, waits for them, and re-layouts  91 us (49%)
  blocking collectives  38.4 us (21%)
  other arithmetic  36.7 us (20%)
  starting transfers between devices  14.3 us (8%)
  matrix products  2.9 us (2%)
    all_gather x1, blocking collectives, collect(): gathered = lax.all_gather(column, 'gx', axis=0, tiled=True)  33 us
    gather x13, local copies, waits for them, and re-layouts, kept_sources(): level_ids = jnp.take_along_axis(paired, node_order, axis=1)  14.6 us
    convert_element_type x1, other arithmetic, local(): return (flux_full.astype(jnp.bfloat16), kept_rows)  12.4 us
    broadcast_in_dim x2, local copies, waits for them, and re-layouts, neighbour(): jnp.where(column == 0, padded[..., 1:-1, :1], jnp.roll(centre, 1, -1))  10.1 us
    broadcast_in_dim x2, local copies, waits for them, and re-layouts, neighbour(): jnp.where(column == width_y - 1, padded[..., 1:-1, -1:], jnp.roll(centre,...  9.91 us
    ppermute x4, starting transfers between devices, padded_2(): lax.ppermute(lax.slice_in_dim(block, 0, width, axis=dim), axis, backward)  9.59 us
    slice x3, local copies, waits for them, and re-layouts, padded_2(): lax.slice_in_dim(block, 0, width, axis=dim)  7.74 us
    gather x1, local copies, waits for them, and re-layouts, collect(): flat_rows[kept_ids.reshape(-1)]  7.62 us
  transfers between devices with their start and end apart: 8, of which 1 were waited for; matrix products, arithmetic and copies ran while one was open for 35% of the time, Pallas kernels for 0%

commit v1 on v0

v1 whole, which is shorter than its diff:
```python
import functools

import jax
import jax.numpy as jnp
from jax import lax
from jax.experimental import pallas as pl
from jax.experimental.pallas import tpu as pltpu
from jax.sharding import PartitionSpec as P

MESH = pl.DeviceIdType.MESH
F32 = jnp.float32
BF16 = jnp.bfloat16
CHUNKS = 4


def remote(src, dst, send, recv, device):
    return pltpu.make_async_remote_copy(
        src_ref=src, dst_ref=dst, send_sem=send, recv_sem=recv, device_id=device, device_id_type=MESH
    )


def kernel(
    ngx, ngy, k_count, planes, cx, cy,
    states, classes, perm, cands, order, flux_out, kept_out,
    st32, flux32, ksc, tx, ty, tz, xs, xr, kxs, kxr, ys, yr, tcol, ordt, onehot, g1, g2,
    xsend, xrecv, ysend, yrecv, g1send, g1recv, g2send, g2recv, sibsend, sibrecv,
):
    a = lax.axis_index("gx")
    b = lax.axis_index("gy")
    zx = planes * cx
    nodes = ngx * ngy - 1
    per = k_count // CHUNKS
    half = ngy // 4

    barrier = pltpu.get_barrier_semaphore()
    for d in range(1, ngx):
        pl.semaphore_signal(barrier, inc=1, device_id=(lax.rem(a + d, ngx), b), device_id_type=MESH)
    for d in range(1, ngy):
        pl.semaphore_signal(barrier, inc=1, device_id=(a, lax.rem(b + d, ngy)), device_id_type=MESH)

    def to_perm(ids):
        total = jnp.zeros(ids.shape, F32)
        for c in range(perm.shape[0]):
            total = total + jnp.where(ids == c, perm[c], 0.0)
        return total

    k_here = to_perm(classes[...])
    ksc[...] = k_here
    kxs[0] = ksc[pl.ds(0, planes, stride=cx), :]
    kxs[1] = ksc[pl.ds(cx - 1, planes, stride=cx), :]
    x_dev = ((lax.rem(a + ngx - 1, ngx), b), (lax.rem(a + 1, ngx), b))
    y_dev = ((a, lax.rem(b + ngy - 1, ngy)), (a, lax.rem(b + 1, ngy)))

    def x_copy(side, c):
        return remote(xs.at[side, c], xr.at[1 - side, c], xsend.at[side, c], xrecv.at[1 - side, c], x_dev[side])

    def kx_copy(side):
        return remote(
            kxs.at[side], kxr.at[1 - side], xsend.at[side, CHUNKS], xrecv.at[1 - side, CHUNKS], x_dev[side]
        )

    def y_copy(side):
        return remote(ys.at[side], yr.at[1 - side], ysend.at[side], yrecv.at[1 - side], y_dev[side])

    def widen(c):
        def pair(i, carry):
            s0 = c * per + 2 * i
            for q in range(2):
                rows = states[q, pl.ds(pl.multiple_of(s0 * zx, 2 * zx), 2 * zx), :].astype(F32)
                st32[q, pl.ds(pl.multiple_of(s0 * zx, 2 * zx), 2 * zx), :] = rows
                to = pl.ds(pl.multiple_of(q * per * planes + i * 2 * planes, 2 * planes), 2 * planes)
                for side, x in ((0, 0), (1, cx - 1)):
                    edge = st32[q, pl.ds(s0 * zx + x, 2 * planes, stride=cx), :]
                    xs[side, c, to, :] = edge.astype(BF16)
            return carry

        lax.fori_loop(0, per // 2, pair, 0)

    widen(0)
    pl.semaphore_wait(barrier, ngx + ngy - 2)
    for side in range(2):
        kx_copy(side).start()
        x_copy(side, 0).start()
    for c in range(1, CHUNKS):
        widen(c)
        for side in range(2):
            x_copy(side, c).start()

    wide = 8 * zx
    pick_row = lax.broadcasted_iota(jnp.int32, (16, cy), 0)
    pick_lane = lax.broadcasted_iota(jnp.int32, (16, cy), 1)
    first = jnp.where((pick_row == 0) & (pick_lane == 0), 1.0, 0.0)
    last = jnp.where((pick_row == 1) & (pick_lane == cy - 1), 1.0, 0.0)
    pick = (first + last).astype(BF16)
    nt = (((1,), (1,)), ((), ()))
    for j in range(k_count // 8):
        for q in range(2):
            cols = lax.dot_general(pick, states[q, j * wide : (j + 1) * wide, :], nt, preferred_element_type=F32)
            ys[0, q, j : j + 1, :] = cols[0:1, :]
            ys[1, q, j : j + 1, :] = cols[1:2, :]
    ids = classes[...].astype(F32).astype(BF16)
    cols = lax.dot_general(pick, jnp.concatenate([ids] * 8, axis=0), nt, preferred_element_type=F32)
    for side in range(2):
        ys[side, 2] = jnp.broadcast_to(to_perm(cols[side : side + 1, :]), (8, wide))
    for side in range(2):
        y_copy(side).start()

    def transmit(k0, k1):
        return k0 * k1 / (k0 + k1)

    cube = (planes, cx, cy)
    k3 = k_here.reshape(cube)
    sub = lax.broadcasted_iota(jnp.int32, cube, 1)
    lane = lax.broadcasted_iota(jnp.int32, cube, 2)
    tx[...] = jnp.where(sub == cx - 1, 0.0, transmit(k3, pltpu.roll(k3, cx - 1, axis=1)))
    ty[...] = jnp.where(lane == cy - 1, 0.0, transmit(k3, pltpu.roll(k3, cy - 1, axis=2)))
    tz[...] = transmit(k3[:-1], k3[1:])

    def inner(s, carry):
        at = pl.ds(pl.multiple_of(s * zx, zx), zx)
        p = st32[0, at, :].reshape(cube)
        sat = st32[1, at, :].reshape(cube)
        m = sat * sat
        fx = tx[...] * (m + pltpu.roll(m, cx - 1, axis=1)) * (pltpu.roll(p, cx - 1, axis=1) - p)
        fy = ty[...] * (m + pltpu.roll(m, cy - 1, axis=2)) * (pltpu.roll(p, cy - 1, axis=2) - p)
        fz = tz[...] * (m[:-1] + m[1:]) * (p[1:] - p[:-1])
        total = (fx - pltpu.roll(fx, 1, axis=1)) + (fy - pltpu.roll(fy, 1, axis=2))
        zero = jnp.zeros((1, cx, cy), F32)
        total = total + (jnp.concatenate([fz, zero], axis=0) - jnp.concatenate([zero, fz], axis=0))
        flux32[at, :] = total.reshape(zx, cy)
        return carry

    lax.fori_loop(0, k_count, inner, 0)

    ordt[...] = jnp.zeros(ordt.shape, F32)
    ordt[0:nodes, :] = order[...].astype(F32)
    turned = ordt[...].T
    spots = lax.broadcasted_iota(jnp.int32, (k_count, 2 * k_count), 1).astype(F32)
    for n in range(nodes):
        onehot[n] = jnp.where(turned[:k_count, n : n + 1] == spots, 1.0, 0.0).astype(BF16)

    for side in range(2):
        y_copy(side).wait_recv()
    for side in range(2):
        mine, theirs = ys[side, 1], yr[side, 1]
        step = yr[side, 0] - ys[side, 0]
        face = transmit(ys[side, 2], yr[side, 2]) * (mine * mine + theirs * theirs) * step
        tcol[side] = face.T

    for side in range(2):
        kx_copy(side).wait_recv()
    kedge = [transmit(kxs[side], kxr[side]) for side in range(2)]
    kedge = [jnp.concatenate([one, one], axis=0) for one in kedge]
    lane2 = lax.broadcasted_iota(jnp.int32, (2 * zx, cy), 1)
    for c in range(CHUNKS):
        for side in range(2):
            x_copy(side, c).wait_recv()

        for j in range(c * per // 8, (c + 1) * per // 8):
            def outer(i, carry, j=j, c=c):
                s0 = j * 8 + 2 * i
                local = s0 - c * per
                at = pl.ds(pl.multiple_of(s0 * zx, 2 * zx), 2 * zx)
                for side, x in ((0, 0), (1, cx - 1)):
                    rp = pl.ds(pl.multiple_of(local * planes, 2 * planes), 2 * planes)
                    rs = pl.ds(pl.multiple_of((per + local) * planes, 2 * planes), 2 * planes)
                    p0, s_0 = xs[side, c, rp, :].astype(F32), xs[side, c, rs, :].astype(F32)
                    p1, s_1 = xr[side, c, rp, :].astype(F32), xr[side, c, rs, :].astype(F32)
                    face = kedge[side] * (s_0 * s_0 + s_1 * s_1) * (p1 - p0)
                    rows = pl.ds(s0 * zx + x, 2 * planes, stride=cx)
                    flux32[rows, :] = flux32[rows, :] + face
                tat = pl.ds(pl.multiple_of(2 * i * zx, 2 * zx), 2 * zx)
                total = flux32[at, :]
                total = total + jnp.where(lane2 == 0, tcol[0, tat, j : j + 1], 0.0)
                total = total + jnp.where(lane2 == cy - 1, tcol[1, tat, j : j + 1], 0.0)
                flux32[at, :] = total
                flux_out[at, :] = total.astype(BF16)
                return carry

            lax.fori_loop(0, 4, outer, 0)

    lane_k = lax.broadcasted_iota(jnp.int32, (k_count, cy), 1)

    def take(i8, acc):
        for u in range(8):
            i = i8 * 8 + u
            cell = cands[a, b, i]
            row = lax.div(cell, cy)
            col = cell - row * cy
            found = flux32[pl.ds(row, k_count, stride=zx), :]
            value = jnp.sum(jnp.where(lane_k == col, found, 0.0), axis=1, keepdims=True)
            acc = jnp.where(lane_k == i, value, acc)
        return acc

    picked = lax.fori_loop(0, k_count // 8, take, jnp.zeros((k_count, cy), F32)).T[:k_count]
    high = picked.astype(BF16).astype(F32)
    mine = jnp.concatenate([high, picked - high], axis=1).astype(BF16)
    g1[b] = mine

    def g1_copy(d, slot, device):
        return remote(g1.at[slot], g1.at[slot], g1send.at[d], g1recv.at[d], device)

    for d in range(1, ngy):
        g1_copy(d, b, (a, lax.rem(b + d, ngy))).start()
    for d in range(1, ngy):
        g1_copy(d, lax.rem(b + ngy - d, ngy), (a, lax.rem(b + d, ngy))).wait_recv()

    def merge(hot, upper, lower):
        stack = jnp.concatenate([upper, lower], axis=0)
        return jnp.dot(hot, stack, preferred_element_type=F32)

    groups = ngy // 2
    for j in range(groups):
        kept = merge(onehot[a * groups + j], g1[2 * j], g1[2 * j + 1])
        g2[a, j] = kept.astype(BF16)
    core = lax.rem(b, 2)
    twin = (a, b + 1 - 2 * core)
    own = pl.ds(core * half, half)
    other = pl.ds((1 - core) * half, half)

    def g2_copy(d, slot, device):
        return remote(g2.at[slot, own], g2.at[slot, own], g2send.at[d], g2recv.at[d], device)

    def sib_copy(d, slot, part):
        return remote(g2.at[slot, part], g2.at[slot, part], sibsend.at[d], sibrecv.at[d], twin)

    for d in range(1, ngx):
        g2_copy(d, a, (lax.rem(a + d, ngx), b)).start()
    for d in range(1, ngx):
        slot = lax.rem(a + ngx - d, ngx)
        g2_copy(d, slot, (lax.rem(a + d, ngx), b)).wait_recv()
        sib_copy(d, slot, own).start()
    for d in range(1, ngx):
        sib_copy(d, lax.rem(a + ngx - d, ngx), other).wait_recv()

    level = []
    for n in range(ngx * groups):
        rows = g2[n // groups, n % groups]
        level.append(rows)
        wide_rows = rows.astype(F32)
        kept_out[n] = wide_rows[:, :k_count] + wide_rows[:, k_count:]
    n = ngx * groups
    while len(level) > 1:
        following = []
        for j in range(len(level) // 2):
            kept = merge(onehot[n], level[2 * j], level[2 * j + 1])
            kept_out[n] = kept[:, :k_count] + kept[:, k_count:]
            following.append(kept.astype(BF16))
            n += 1
        level = following

    for side in range(2):
        kx_copy(side).wait_send()
        y_copy(side).wait_send()
        for c in range(CHUNKS):
            x_copy(side, c).wait_send()
    for d in range(1, ngy):
        g1_copy(d, b, (a, lax.rem(b + d, ngy))).wait_send()
    for d in range(1, ngx):
        g2_copy(d, a, (lax.rem(a + d, ngx), b)).wait_send()
        sib_copy(d, lax.rem(a + ngx - d, ngx), own).wait_send()


def solution(mesh):
    ngx, ngy = mesh.shape["gx"], mesh.shape["gy"]

    def local(states, class_map, perm_table, candidates, merge_order):
        _, k, planes, cx, cy = states.shape
        zx = planes * cx
        nodes = merge_order.shape[0]
        padded = (nodes + 7) // 8 * 8
        edge = 2 * (k // CHUNKS) * planes
        vmem = pl.BlockSpec(memory_space=pltpu.VMEM)
        smem = pl.BlockSpec(memory_space=pltpu.SMEM)
        dma = pltpu.SemaphoreType.DMA
        flux, kept = pl.pallas_call(
            functools.partial(kernel, ngx, ngy, k, planes, cx, cy),
            out_shape=(
                jax.ShapeDtypeStruct((k * zx, cy), BF16),
                jax.ShapeDtypeStruct((nodes, k, k), F32),
            ),
            in_specs=[vmem, vmem, smem, smem, vmem],
            out_specs=(vmem, vmem),
            scratch_shapes=[
                pltpu.VMEM((2, k * zx, cy), F32),
                pltpu.VMEM((k * zx, cy), F32),
                pltpu.VMEM((zx, cy), F32),
                pltpu.VMEM((planes, cx, cy), F32),
                pltpu.VMEM((planes, cx, cy), F32),
                pltpu.VMEM((planes - 1, cx, cy), F32),
                pltpu.VMEM((2, CHUNKS, edge, cy), BF16),
                pltpu.VMEM((2, CHUNKS, edge, cy), BF16),
                pltpu.VMEM((2, planes, cy), F32),
                pltpu.VMEM((2, planes, cy), F32),
                pltpu.VMEM((2, 3, k // 8, 8 * zx), F32),
                pltpu.VMEM((2, 3, k // 8, 8 * zx), F32),
                pltpu.VMEM((2, 8 * zx, k // 8), F32),
                pltpu.VMEM((padded, 2 * k), F32),
                pltpu.VMEM((nodes, k, 2 * k), BF16),
                pltpu.VMEM((ngy, k, 2 * k), BF16),
                pltpu.VMEM((ngx, ngy // 2, k, 2 * k), BF16),
                dma((2, CHUNKS + 1)),
                dma((2, CHUNKS + 1)),
                dma((2,)),
                dma((2,)),
                dma((ngy,)),
                dma((ngy,)),
                dma((ngx,)),
                dma((ngx,)),
                dma((ngx,)),
                dma((ngx,)),
            ],
            compiler_params=pltpu.CompilerParams(
                collective_id=0, has_side_effects=True, vmem_limit_bytes=48 * 1024 * 1024
            ),
        )(states.reshape(2, k * zx, cy), class_map.reshape(zx, cy), perm_table, candidates, merge_order)
        return flux.reshape(k, planes, cx, cy), kept

    in_specs = (P(None, None, None, "gx", "gy"), P(None, "gx", "gy"), P(), P(), P())
    out_specs = (P(None, None, "gx", "gy"), P())
    return jax.shard_map(local, mesh=mesh, in_specs=in_specs, out_specs=out_specs, check_vma=False)
```

time: 187 us -> 41.4 us (0.22)
  local copies, waits for them, and re-layouts: 91 us -> 6.36 us
  blocking collectives: 38.4 us -> 0 us
  other arithmetic: 36.7 us -> 0 us
  Pallas kernels: 0 us -> 33.7 us
  starting transfers between devices: 14.3 us -> 0 us
  matrix products: 2.9 us -> 0 us
    all_gather x2 -> x0, blocking collectives: 38.4 us -> none  [the longest x1 33 us: collect(): gathered = lax.all_gather(column, 'gx', axis=0, tiled=True)]
    slice x21 -> x0, local copies, waits for them, and re-layouts: 35.2 us -> none  [the longest x3 7.74 us: padded_2(): lax.slice_in_dim(block, 0, width, axis=dim)]
    pallas_call x0 -> x1, Pallas kernels: none -> 33.7 us  [local(): pl.pallas_call(functools.partial(kernel, ngx, ngy, k, planes, cx, cy), ou...]
    gather x14 -> x0, local copies, waits for them, and re-layouts: 22.2 us -> none  [the longest x13 14.6 us: kept_sources(): level_ids = jnp.take_along_axis(paired, node_order, axis=1)]
    broadcast_in_dim x6 -> x0, local copies, waits for them, and re-layouts: 21.7 us -> none  [the longest x2 10.1 us: neighbour(): jnp.where(column == 0, padded[..., 1:-1, :1], jnp.roll(centre, 1, -1))]
    ppermute x8 -> x0, starting transfers between devices: 14.3 us -> none  [the longest x4 9.59 us: padded_2(): lax.ppermute(lax.slice_in_dim(block, 0, width, axis=dim), axis, backward)]
    convert_element_type x1 -> x0, other arithmetic: 12.4 us -> none  [local(): return (flux_full.astype(jnp.bfloat16), kept_rows)]
    add x2 -> x0, other arithmetic: 10.2 us -> none  [the longest x1 5.14 us: local(): perm_pad + jnp.where(class_pad == class_num, perm_table[class_num], 0.0)]
  transfers between devices with their start and end apart: 8 -> 0, of which waited for: 1 -> 0; matrix products, arithmetic and copies ran while one was open for 35% -> 0% of each run, Pallas kernels for 0% -> 0%
where the time goes in v1:
time: 41.4 us; the launch traced here: 40.7 us
  Pallas kernels  33.7 us (81%)
  local copies, waits for them, and re-layouts  6.36 us (15%)
  between operations  0.65 us (2%)
    pallas_call x1, Pallas kernels, local(): pl.pallas_call(functools.partial(kernel, ngx, ngy, k, planes, cx, cy), ou...  33.7 us
    unnamed x12, local copies, waits for them, and re-layouts  6.36 us

profile of v1, /device:TPU:0, one launch (start us, length us, event | category | flops | bytes accessed | tf_op | source)
XLA Modules:
  0.0 40.7 jit_solution(12250000416766114382)
XLA Ops:
  0.6 0.0 copy-start
  0.6 1.6 %copy-done = bf16[2,64,8,8,128]{4,3,2,1,0:T(8,128)(2,1)S(1)} copy-done((bf16[2,64,8,8,128]{4,3,2,1,0:T(8,128)(2,1)S(1)}, bf16[2,64,8,8,128]{4,3,2,1,0:T(8,128)(2,1)}, u32[]{:S(2)}) %copy-start) | copy-done | bytes 2097176
  2.2 0.0 copy-start.1
  2.2 0.8 %copy-done.1 = s32[8,8,128]{2,1,0:T(8,128)S(1)} copy-done((s32[8,8,128]{2,1,0:T(8,128)S(1)}, s32[8,8,128]{2,1,0:T(8,128)}, u32[]{:S(2)}) %copy-start.1) | copy-done | bytes 32792
  3.0 0.0 copy-start.2
  3.0 0.7 %copy-done.2 = s32[8,4,64]{2,1,0:T(4,128)S(1)} copy-done((s32[8,4,64]{2,1,0:T(4,128)S(1)}, s32[8,4,64]{2,1,0:T(4,128)}, u32[]{:S(2)}) %copy-start.2) | copy-done | bytes 8216
  3.7 0.0 copy-start.3
  3.7 0.7 %copy-done.3 = s32[31,128]{1,0:T(8,128)S(1)} copy-done((s32[31,128]{1,0:T(8,128)S(1)}, s32[31,128]{1,0:T(8,128)}, u32[]{:S(2)}) %copy-start.3) | copy-done | bytes 15896
  4.4 0.0 copy-start.4
  4.4 0.7 %copy-done.4 = f32[8]{0:T(128)S(1)} copy-done((f32[8]{0:T(128)S(1)}, f32[8]{0:T(128)}, u32[]{:S(2)}) %copy-start.4) | copy-done | bytes 56
  5.1 33.7 %shard_map.68 = (bf16[4096,128]{1,0:T(8,128)(2,1)S(1)}, f32[31,64,64]{2,1,0:T(8,128)S(1)}) custom-call(bf16[2,4096,128]{2,1,0:T(8,128)(2,1)S(1)} %bitcast.3, s32[64,128]{1,0:T(8,128)S(1)} %bitcast.5, f32[8]{0:T(128)S(1)} %copy-done.4, s32[8,4,64]{2,1,0:T(4,128)S(1)} %copy-done.2, s32[31,128]{1,0:T(8,128)S(1)} %copy-done.3), custom_call_target="tpu_custom_call" | custom-call | tf_op jit(solution)/shard_map/pallas_call | solution.py:276
  38.8 1.0 %copy.9 = bf16[64,8,8,128]{3,2,1,0:T(8,128)(2,1)} copy(bf16[64,8,8,128]{3,2,1,0:T(8,128)(2,1)S(1)} %bitcast.4) | data formatting | bytes 2097152
  39.8 1.0 %copy.10 = f32[31,64,64]{2,1,0:T(8,128)} copy(f32[31,64,64]{2,1,0:T(8,128)S(1)} %get-tuple-element.9) | data formatting | bytes 1015808
Async XLA Ops:
  0.6 1.6 %copy-start = (bf16[2,64,8,8,128]{4,3,2,1,0:T(8,128)(2,1)S(1)}, bf16[2,64,8,8,128]{4,3,2,1,0:T(8,128)(2,1)}, u32[]{:S(2)}) copy-start(bf16[2,64,8,8,128]{4,3,2,1,0:T(8,128)(2,1)} %param.5) | copy-start | bytes 6291460
  2.2 0.8 %copy-start.1 = (s32[8,8,128]{2,1,0:T(8,128)S(1)}, s32[8,8,128]{2,1,0:T(8,128)}, u32[]{:S(2)}) copy-start(s32[8,8,128]{2,1,0:T(8,128)} %param.6) | copy-start | bytes 98308
  3.0 0.7 %copy-start.2 = (s32[8,4,64]{2,1,0:T(4,128)S(1)}, s32[8,4,64]{2,1,0:T(4,128)}, u32[]{:S(2)}) copy-start(s32[8,4,64]{2,1,0:T(4,128)} %cands.1) | copy-start | bytes 24580
  3.7 0.7 %copy-start.3 = (s32[31,128]{1,0:T(8,128)S(1)}, s32[31,128]{1,0:T(8,128)}, u32[]{:S(2)}) copy-start(s32[31,128]{1,0:T(8,128)} %order.1) | copy-start | bytes 47620
  4.4 0.7 %copy-start.4 = (f32[8]{0:T(128)S(1)}, f32[8]{0:T(128)}, u32[]{:S(2)}) copy-start(f32[8]{0:T(128)} %perm.1) | copy-start | bytes 100

commit v2 on v1

--- a/solution.py
+++ b/solution.py
@@ -21,7 +21,8 @@
 
 def kernel(
     ngx, ngy, k_count, planes, cx, cy,
-    states, classes, perm, cands, order, flux_out, kept_out,
+    states_in, classes_in, perm_in, cands_in, order_in, flux_out, kept_out,
+    states, classes, perm, cands, order, rowst, insem,
     st32, flux32, ksc, tx, ty, tz, xs, xr, kxs, kxr, ys, yr, tcol, ordt, onehot, g1, g2,
     xsend, xrecv, ysend, yrecv, g1send, g1recv, g2send, g2recv, sibsend, sibrecv,
 ):
@@ -32,6 +33,20 @@
     per = k_count // CHUNKS
     half = ngy // 4
 
+    def load(c):
+        rows = pl.ds(c * per * zx, per * zx)
+        return pltpu.make_async_copy(states_in.at[:, rows], states.at[:, rows], insem.at[c])
+
+    pairs = ((classes_in, classes), (perm_in, perm), (cands_in, cands), (order_in, order))
+    small = [pltpu.make_async_copy(src, dst, insem.at[CHUNKS + i]) for i, (src, dst) in enumerate(pairs)]
+    load(0).start()
+    small[0].start()
+    small[1].start()
+    for c in range(1, CHUNKS):
+        load(c).start()
+    small[2].start()
+    small[3].start()
+
     barrier = pltpu.get_barrier_semaphore()
     for d in range(1, ngx):
         pl.semaphore_signal(barrier, inc=1, device_id=(lax.rem(a + d, ngx), b), device_id_type=MESH)
@@ -44,6 +59,8 @@
             total = total + jnp.where(ids == c, perm[c], 0.0)
         return total
 
+    small[0].wait()
+    small[1].wait()
     k_here = to_perm(classes[...])
     ksc[...] = k_here
     kxs[0] = ksc[pl.ds(0, planes, stride=cx), :]
@@ -74,14 +91,16 @@
                     xs[side, c, to, :] = edge.astype(BF16)
             return carry
 
-        lax.fori_loop(0, per // 2, pair, 0)
-
+        lax.fori_loop(0, per // 2, pair, 0, unroll=2)
+
+    load(0).wait()
     widen(0)
     pl.semaphore_wait(barrier, ngx + ngy - 2)
     for side in range(2):
         kx_copy(side).start()
         x_copy(side, 0).start()
     for c in range(1, CHUNKS):
+        load(c).wait()
         widen(c)
         for side in range(2):
             x_copy(side, c).start()
@@ -130,8 +149,10 @@
         flux32[at, :] = total.reshape(zx, cy)
         return carry
 
-    lax.fori_loop(0, k_count, inner, 0)
-
+    lax.fori_loop(0, k_count, inner, 0, unroll=2)
+
+    small[3].wait()
+    small[2].wait()
     ordt[...] = jnp.zeros(ordt.shape, F32)
     ordt[0:nodes, :] = order[...].astype(F32)
     turned = ordt[...].T
@@ -152,6 +173,7 @@
     kedge = [transmit(kxs[side], kxr[side]) for side in range(2)]
     kedge = [jnp.concatenate([one, one], axis=0) for one in kedge]
     lane2 = lax.broadcasted_iota(jnp.int32, (2 * zx, cy), 1)
+    lane_k = lax.broadcasted_iota(jnp.int32, (per, cy), 1)
     for c in range(CHUNKS):
         for side in range(2):
             x_copy(side, c).wait_recv()
@@ -160,16 +182,16 @@
             def outer(i, carry, j=j, c=c):
                 s0 = j * 8 + 2 * i
                 local = s0 - c * per
-                at = pl.ds(pl.multiple_of(s0 * zx, 2 * zx), 2 * zx)
+                at = pl.ds(s0 * zx, 2 * zx)
                 for side, x in ((0, 0), (1, cx - 1)):
-                    rp = pl.ds(pl.multiple_of(local * planes, 2 * planes), 2 * planes)
-                    rs = pl.ds(pl.multiple_of((per + local) * planes, 2 * planes), 2 * planes)
+                    rp = pl.ds(local * planes, 2 * planes)
+                    rs = pl.ds((per + local) * planes, 2 * planes)
                     p0, s_0 = xs[side, c, rp, :].astype(F32), xs[side, c, rs, :].astype(F32)
                     p1, s_1 = xr[side, c, rp, :].astype(F32), xr[side, c, rs, :].astype(F32)
                     face = kedge[side] * (s_0 * s_0 + s_1 * s_1) * (p1 - p0)
                     rows = pl.ds(s0 * zx + x, 2 * planes, stride=cx)
                     flux32[rows, :] = flux32[rows, :] + face
-                tat = pl.ds(pl.multiple_of(2 * i * zx, 2 * zx), 2 * zx)
+                tat = pl.ds(2 * i * zx, 2 * zx)
                 total = flux32[at, :]
                 total = total + jnp.where(lane2 == 0, tcol[0, tat, j : j + 1], 0.0)
                 total = total + jnp.where(lane2 == cy - 1, tcol[1, tat, j : j + 1], 0.0)
@@ -177,22 +199,22 @@
                 flux_out[at, :] = total.astype(BF16)
                 return carry
 
-            lax.fori_loop(0, 4, outer, 0)
-
-    lane_k = lax.broadcasted_iota(jnp.int32, (k_count, cy), 1)
-
-    def take(i8, acc):
-        for u in range(8):
-            i = i8 * 8 + u
-            cell = cands[a, b, i]
-            row = lax.div(cell, cy)
-            col = cell - row * cy
-            found = flux32[pl.ds(row, k_count, stride=zx), :]
-            value = jnp.sum(jnp.where(lane_k == col, found, 0.0), axis=1, keepdims=True)
-            acc = jnp.where(lane_k == i, value, acc)
-        return acc
-
-    picked = lax.fori_loop(0, k_count // 8, take, jnp.zeros((k_count, cy), F32)).T[:k_count]
+            for i in range(4):
+                outer(i, 0)
+
+        def take(i16, acc, c=c):
+            for u in range(16):
+                i = i16 * 16 + u
+                cell = cands[a, b, i]
+                row = lax.div(cell, cy)
+                found = flux32[pl.ds(c * per * zx + row, per, stride=zx), :]
+                value = jnp.sum(jnp.where(lane_k == cell - row * cy, found, 0.0), axis=1, keepdims=True)
+                acc = jnp.where(lane_k == i, value, acc)
+            return acc
+
+        rowst[c * per : (c + 1) * per, :] = lax.fori_loop(0, k_count // 16, take, jnp.zeros((per, cy), F32))
+
+    picked = rowst[...].T[:k_count]
     high = picked.astype(BF16).astype(F32)
     mine = jnp.concatenate([high, picked - high], axis=1).astype(BF16)
     g1[b] = mine
@@ -271,7 +293,7 @@
         padded = (nodes + 7) // 8 * 8
         edge = 2 * (k // CHUNKS) * planes
         vmem = pl.BlockSpec(memory_space=pltpu.VMEM)
-        smem = pl.BlockSpec(memory_space=pltpu.SMEM)
+        hbm = pl.BlockSpec(memory_space=pltpu.HBM)
         dma = pltpu.SemaphoreType.DMA
         flux, kept = pl.pallas_call(
             functools.partial(kernel, ngx, ngy, k, planes, cx, cy),
@@ -279,9 +301,16 @@
                 jax.ShapeDtypeStruct((k * zx, cy), BF16),
                 jax.ShapeDtypeStruct((nodes, k, k), F32),
             ),
-            in_specs=[vmem, vmem, smem, smem, vmem],
+            in_specs=[hbm] * 5,
             out_specs=(vmem, vmem),
             scratch_shapes=[
+                pltpu.VMEM((2, k * zx, cy), BF16),
+                pltpu.VMEM((zx, cy), jnp.int32),
+                pltpu.SMEM(perm_table.shape, F32),
+                pltpu.SMEM(candidates.shape, jnp.int32),
+                pltpu.VMEM((nodes, 2 * k), jnp.int32),
+                pltpu.VMEM((k, cy), F32),
+                dma((CHUNKS + 4,)),
                 pltpu.VMEM((2, k * zx, cy), F32),
                 pltpu.VMEM((k * zx, cy), F32),
                 pltpu.VMEM((zx, cy), F32),
@@ -313,7 +342,10 @@
             compiler_params=pltpu.CompilerParams(
                 collective_id=0, has_side_effects=True, vmem_limit_bytes=48 * 1024 * 1024
             ),
-        )(states.reshape(2, k * zx, cy), class_map.reshape(zx, cy), perm_table, candidates, merge_order)
+        )(*(
+            pltpu.with_memory_space_constraint(x, pltpu.HBM)
+            for x in (states.reshape(2, k * zx, cy), class_map.reshape(zx, cy), perm_table, candidates, merge_order)
+        ))
         return flux.reshape(k, planes, cx, cy), kept
 
     in_specs = (P(None, None, None, "gx", "gy"), P(None, "gx", "gy"), P(), P(), P())

time: 41.4 us -> 32.3 us (0.78)
  the two profiles are of different devices: /device:TPU:0 before, /device:TPU:1 now
where the time goes in v2:
time: 32.3 us; the launch traced here: 32.2 us
  Pallas kernels  29.6 us (92%)
  local copies, waits for them, and re-layouts  1.93 us (6%)
  between operations  0.64 us (2%)
    pallas_call x1, Pallas kernels, local(): pl.pallas_call(functools.partial(kernel, ngx, ngy, k, planes, cx, cy), ou...  29.6 us
    unnamed x2, local copies, waits for them, and re-layouts  1.93 us

profile of v2, /device:TPU:1, one launch (start us, length us, event | category | flops | bytes accessed | tf_op | source)
XLA Modules:
  0.0 32.2 jit_solution(14577297883099756162)
XLA Ops:
  0.6 29.6 %shard_map.68 = (bf16[4096,128]{1,0:T(8,128)(2,1)S(1)}, f32[31,64,64]{2,1,0:T(8,128)S(1)}) custom-call(bf16[2,4096,128]{2,1,0:T(8,128)(2,1)} %bitcast.4, s32[64,128]{1,0:T(8,128)} %bitcast.5, f32[8]{0:T(128)} %perm_in.1, s32[8,4,64]{2,1,0:T(4,128)} %cands_in.1, s32[31,128]{1,0:T(8,128)} %order_in.1), custom_call_target="tpu_custom_call" | custom-call | tf_op jit(solution)/shard_map/pallas_call | solution.py:298
  30.3 1.0 %copy.9 = bf16[64,8,8,128]{3,2,1,0:T(8,128)(2,1)} copy(bf16[64,8,8,128]{3,2,1,0:T(8,128)(2,1)S(1)} %bitcast.3) | data formatting | bytes 2097152
  31.2 1.0 %copy.10 = f32[31,64,64]{2,1,0:T(8,128)} copy(f32[31,64,64]{2,1,0:T(8,128)S(1)} %get-tuple-element.9) | data formatting | bytes 1015808

commit v3 on v2

--- a/solution.py
+++ b/solution.py
@@ -19,11 +19,47 @@
     )
 
 
+def merge(hot, upper, lower):
+    stack = jnp.concatenate([upper, lower], axis=0)
+    return jnp.dot(hot, stack, preferred_element_type=F32)
+
+
+def finish(k_count, flux_in, g2, hots, flux_out, kept_out, kept, sems):
+    ngx, groups = g2.shape[:2]
+    first = ngx * groups
+    put_flux = pltpu.make_async_copy(flux_in, flux_out, sems.at[0])
+    put_flux.start()
+    level = []
+    for n in range(first):
+        rows = g2[n // groups, n % groups]
+        level.append(rows)
+        wide_rows = rows.astype(F32)
+        kept[n] = wide_rows[:, :k_count] + wide_rows[:, k_count:]
+    put_low = pltpu.make_async_copy(kept.at[pl.ds(0, first)], kept_out.at[pl.ds(0, first)], sems.at[1])
+    put_low.start()
+    n = first
+    while len(level) > 1:
+        following = []
+        for j in range(len(level) // 2):
+            rows = merge(hots[n - first], level[2 * j], level[2 * j + 1])
+            kept[n] = rows[:, :k_count] + rows[:, k_count:]
+            following.append(rows.astype(BF16))
+            n += 1
+        level = following
+    put_high = pltpu.make_async_copy(
+        kept.at[pl.ds(first, n - first)], kept_out.at[pl.ds(first, n - first)], sems.at[2]
+    )
+    put_high.start()
+    put_flux.wait()
+    put_low.wait()
+    put_high.wait()
+
+
 def kernel(
     ngx, ngy, k_count, planes, cx, cy,
-    states_in, classes_in, perm_in, cands_in, order_in, flux_out, kept_out,
+    states_in, classes_in, perm_in, cands_in, order_in, flux_out, g2, hots,
     states, classes, perm, cands, order, rowst, insem,
-    st32, flux32, ksc, tx, ty, tz, xs, xr, kxs, kxr, ys, yr, tcol, ordt, onehot, g1, g2,
+    st32, flux32, ksc, tx, ty, tz, xs, xr, kxs, kxr, ys, yr, ky, kyr, yface, ordt, onehot, g1,
     xsend, xrecv, ysend, yrecv, g1send, g1recv, g2send, g2recv, sibsend, sibrecv,
 ):
     a = lax.axis_index("gx")
@@ -77,7 +113,10 @@
         )
 
     def y_copy(side):
-        return remote(ys.at[side], yr.at[1 - side], ysend.at[side], yrecv.at[1 - side], y_dev[side])
+        return remote(ys, yr.at[1 - side], ysend.at[side], yrecv.at[1 - side], y_dev[side])
+
+    def ky_copy(side):
+        return remote(ky, kyr.at[1 - side], ysend.at[2 + side], yrecv.at[3 - side], y_dev[side])
 
     def widen(c):
         def pair(i, carry):
@@ -105,24 +144,30 @@
         for side in range(2):
             x_copy(side, c).start()
 
-    wide = 8 * zx
-    pick_row = lax.broadcasted_iota(jnp.int32, (16, cy), 0)
-    pick_lane = lax.broadcasted_iota(jnp.int32, (16, cy), 1)
-    first = jnp.where((pick_row == 0) & (pick_lane == 0), 1.0, 0.0)
-    last = jnp.where((pick_row == 1) & (pick_lane == cy - 1), 1.0, 0.0)
-    pick = (first + last).astype(BF16)
-    nt = (((1,), (1,)), ((), ()))
-    for j in range(k_count // 8):
-        for q in range(2):
-            cols = lax.dot_general(pick, states[q, j * wide : (j + 1) * wide, :], nt, preferred_element_type=F32)
-            ys[0, q, j : j + 1, :] = cols[0:1, :]
-            ys[1, q, j : j + 1, :] = cols[1:2, :]
-    ids = classes[...].astype(F32).astype(BF16)
-    cols = lax.dot_general(pick, jnp.concatenate([ids] * 8, axis=0), nt, preferred_element_type=F32)
-    for side in range(2):
-        ys[side, 2] = jnp.broadcast_to(to_perm(cols[side : side + 1, :]), (8, wide))
+    lane1 = lax.broadcasted_iota(jnp.int32, (cx, cy), 1)
+
+    def pack(plane):
+        packed = jnp.zeros((cx, cy), F32)
+        for j in range(cy // 2):
+            packed = jnp.where((lane1 == 2 * j) | (lane1 == 2 * j + 1), pltpu.roll(plane(j), 2 * j + 1, axis=1), packed)
+        return packed
+
+    block = cy // 2 * cx
+    blocks = k_count * zx // block
+
+    def pack_block(t, carry):
+        def plane(q):
+            return lambda j: st32[q, pl.ds(pl.multiple_of(t * block, block) + j * cx, cx), :]
+
+        both = jnp.concatenate([pack(plane(0)), pack(plane(1))], axis=0)
+        ys[pl.ds(pl.multiple_of(t * 2 * cx, 2 * cx), 2 * cx), :] = both.astype(BF16)
+        return carry
+
+    lax.fori_loop(0, blocks, pack_block, 0)
+    ky[...] = pack(lambda j: ksc[j % planes * cx : (j % planes + 1) * cx, :])
     for side in range(2):
         y_copy(side).start()
+        ky_copy(side).start()
 
     def transmit(k0, k1):
         return k0 * k1 / (k0 + k1)
@@ -158,21 +203,31 @@
     turned = ordt[...].T
     spots = lax.broadcasted_iota(jnp.int32, (k_count, 2 * k_count), 1).astype(F32)
     for n in range(nodes):
-        onehot[n] = jnp.where(turned[:k_count, n : n + 1] == spots, 1.0, 0.0).astype(BF16)
+        hot = jnp.where(turned[:k_count, n : n + 1] == spots, 1.0, 0.0).astype(BF16)
+        if n < ngx * ngy // 2:
+            onehot[n] = hot
+        else:
+            hots[n - ngx * ngy // 2] = hot
 
     for side in range(2):
         y_copy(side).wait_recv()
-    for side in range(2):
-        mine, theirs = ys[side, 1], yr[side, 1]
-        step = yr[side, 0] - ys[side, 0]
-        face = transmit(ys[side, 2], yr[side, 2]) * (mine * mine + theirs * theirs) * step
-        tcol[side] = face.T
+        ky_copy(side).wait_recv()
+
+    def across(low, high):
+        return jnp.where(lane1 % 2 == 0, pltpu.roll(high, cy - 1, axis=1), pltpu.roll(low, 1, axis=1))
+
+    kcol = transmit(ky[...], across(kyr[0], kyr[1]))
+    for t in range(blocks):
+        rows = pl.ds(t * 2 * cx, 2 * cx)
+        own, low, high = ys[rows, :].astype(F32), yr[0, rows, :].astype(F32), yr[1, rows, :].astype(F32)
+        p1, s_1 = across(low[:cx], high[:cx]), across(low[cx:], high[cx:])
+        yface[t] = kcol * (own[cx:] * own[cx:] + s_1 * s_1) * (p1 - own[:cx])
 
     for side in range(2):
         kx_copy(side).wait_recv()
     kedge = [transmit(kxs[side], kxr[side]) for side in range(2)]
     kedge = [jnp.concatenate([one, one], axis=0) for one in kedge]
-    lane2 = lax.broadcasted_iota(jnp.int32, (2 * zx, cy), 1)
+    rim = (lane1 == 0) | (lane1 == cy - 1)
     lane_k = lax.broadcasted_iota(jnp.int32, (per, cy), 1)
     for c in range(CHUNKS):
         for side in range(2):
@@ -191,10 +246,11 @@
                     face = kedge[side] * (s_0 * s_0 + s_1 * s_1) * (p1 - p0)
                     rows = pl.ds(s0 * zx + x, 2 * planes, stride=cx)
                     flux32[rows, :] = flux32[rows, :] + face
-                tat = pl.ds(2 * i * zx, 2 * zx)
-                total = flux32[at, :]
-                total = total + jnp.where(lane2 == 0, tcol[0, tat, j : j + 1], 0.0)
-                total = total + jnp.where(lane2 == cy - 1, tcol[1, tat, j : j + 1], 0.0)
+                fix = []
+                for v in range(2 * planes):
+                    t, u = divmod(s0 * planes + v, cy // 2)
+                    fix.append(jnp.where(rim, pltpu.roll(yface[t], cy - 1 - 2 * u, axis=1), 0.0))
+                total = flux32[at, :] + jnp.concatenate(fix, axis=0)
                 flux32[at, :] = total
                 flux_out[at, :] = total.astype(BF16)
                 return carry
@@ -227,10 +283,6 @@
     for d in range(1, ngy):
         g1_copy(d, lax.rem(b + ngy - d, ngy), (a, lax.rem(b + d, ngy))).wait_recv()
 
-    def merge(hot, upper, lower):
-        stack = jnp.concatenate([upper, lower], axis=0)
-        return jnp.dot(hot, stack, preferred_element_type=F32)
-
     groups = ngy // 2
     for j in range(groups):
         kept = merge(onehot[a * groups + j], g1[2 * j], g1[2 * j + 1])
@@ -255,25 +307,10 @@
     for d in range(1, ngx):
         sib_copy(d, lax.rem(a + ngx - d, ngx), other).wait_recv()
 
-    level = []
-    for n in range(ngx * groups):
-        rows = g2[n // groups, n % groups]
-        level.append(rows)
-        wide_rows = rows.astype(F32)
-        kept_out[n] = wide_rows[:, :k_count] + wide_rows[:, k_count:]
-    n = ngx * groups
-    while len(level) > 1:
-        following = []
-        for j in range(len(level) // 2):
-            kept = merge(onehot[n], level[2 * j], level[2 * j + 1])
-            kept_out[n] = kept[:, :k_count] + kept[:, k_count:]
-            following.append(kept.astype(BF16))
-            n += 1
-        level = following
-
     for side in range(2):
         kx_copy(side).wait_send()
         y_copy(side).wait_send()
+        ky_copy(side).wait_send()
         for c in range(CHUNKS):
             x_copy(side, c).wait_send()
     for d in range(1, ngy):
@@ -292,17 +329,20 @@
         nodes = merge_order.shape[0]
         padded = (nodes + 7) // 8 * 8
         edge = 2 * (k // CHUNKS) * planes
+        blocks = k * planes // (cy // 2)
         vmem = pl.BlockSpec(memory_space=pltpu.VMEM)
         hbm = pl.BlockSpec(memory_space=pltpu.HBM)
         dma = pltpu.SemaphoreType.DMA
-        flux, kept = pl.pallas_call(
+        tiles = ngx * ngy
+        flux, lowest, hots = pl.pallas_call(
             functools.partial(kernel, ngx, ngy, k, planes, cx, cy),
             out_shape=(
                 jax.ShapeDtypeStruct((k * zx, cy), BF16),
-                jax.ShapeDtypeStruct((nodes, k, k), F32),
+                jax.ShapeDtypeStruct((ngx, ngy // 2, k, 2 * k), BF16),
+                jax.ShapeDtypeStruct((nodes - tiles // 2, k, 2 * k), BF16),
             ),
             in_specs=[hbm] * 5,
-            out_specs=(vmem, vmem),
+            out_specs=(vmem,) * 3,
             scratch_shapes=[
                 pltpu.VMEM((2, k * zx, cy), BF16),
                 pltpu.VMEM((zx, cy), jnp.int32),
@@ -321,17 +361,18 @@
                 pltpu.VMEM((2, CHUNKS, edge, cy), BF16),
                 pltpu.VMEM((2, planes, cy), F32),
                 pltpu.VMEM((2, planes, cy), F32),
-                pltpu.VMEM((2, 3, k // 8, 8 * zx), F32),
-                pltpu.VMEM((2, 3, k // 8, 8 * zx), F32),
-                pltpu.VMEM((2, 8 * zx, k // 8), F32),
+                pltpu.VMEM((2 * blocks * cx, cy), BF16),
+                pltpu.VMEM((2, 2 * blocks * cx, cy), BF16),
+                pltpu.VMEM((cx, cy), F32),
+                pltpu.VMEM((2, cx, cy), F32),
+                pltpu.VMEM((blocks, cx, cy), F32),
                 pltpu.VMEM((padded, 2 * k), F32),
-                pltpu.VMEM((nodes, k, 2 * k), BF16),
+                pltpu.VMEM((tiles // 2, k, 2 * k), BF16),
                 pltpu.VMEM((ngy, k, 2 * k), BF16),
-                pltpu.VMEM((ngx, ngy // 2, k, 2 * k), BF16),
                 dma((2, CHUNKS + 1)),
                 dma((2, CHUNKS + 1)),
-                dma((2,)),
-                dma((2,)),
+                dma((4,)),
+                dma((4,)),
                 dma((ngy,)),
                 dma((ngy,)),
                 dma((ngx,)),
@@ -340,12 +381,23 @@
                 dma((ngx,)),
             ],
             compiler_params=pltpu.CompilerParams(
-                collective_id=0, has_side_effects=True, vmem_limit_bytes=48 * 1024 * 1024
+                collective_id=0, has_side_effects=True, vmem_limit_bytes=32 * 1024 * 1024
             ),
         )(*(
             pltpu.with_memory_space_constraint(x, pltpu.HBM)
             for x in (states.reshape(2, k * zx, cy), class_map.reshape(zx, cy), perm_table, candidates, merge_order)
         ))
+        flux, kept = pl.pallas_call(
+            functools.partial(finish, k),
+            out_shape=(
+                jax.ShapeDtypeStruct((k * zx, cy), BF16),
+                jax.ShapeDtypeStruct((nodes, k, k), F32),
+            ),
+            in_specs=[vmem] * 3,
+            out_specs=(hbm, hbm),
+            scratch_shapes=[pltpu.VMEM((nodes, k, k), F32), dma((3,))],
+            compiler_params=pltpu.CompilerParams(vmem_limit_bytes=24 * 1024 * 1024),
+        )(flux, lowest, hots)
         return flux.reshape(k, planes, cx, cy), kept
 
     in_specs = (P(None, None, None, "gx", "gy"), P(None, "gx", "gy"), P(), P(), P())

time: 32.3 us -> 31.6 us (0.978)
  the two profiles are of different devices: /device:TPU:1 before, /device:TPU:0 now
where the time goes in v3:
time: 31.6 us; the launch traced here: 31.4 us
  Pallas kernels  30.8 us (97%)
  between operations  0.64 us (2%)
    pallas_call x1, Pallas kernels, local(): pl.pallas_call(functools.partial(kernel, ngx, ngy, k, planes, cx, cy), ou...  29.3 us
    pallas_call x1, Pallas kernels, local(): pl.pallas_call(functools.partial(finish, k), out_shape=(jax.ShapeDtypeStr...  1.46 us

profile of v3, /device:TPU:0, one launch (start us, length us, event | category | flops | bytes accessed | tf_op | source)
XLA Modules:
  0.0 31.4 jit_solution(4232756455336808120)
XLA Ops:
  0.6 29.3 %shard_map.68 = (bf16[4096,128]{1,0:T(8,128)(2,1)S(1)}, bf16[8,2,64,128]{3,2,1,0:T(8,128)(2,1)S(1)}, bf16[15,64,128]{2,1,0:T(8,128)(2,1)S(1)}) custom-call(bf16[2,4096,128]{2,1,0:T(8,128)(2,1)} %bitcast.3, s32[64,128]{1,0:T(8,128)} %bitcast.4, f32[8]{0:T(128)} %perm_in.1, s32[8,4,64]{2,1,0:T(4,128)} %cands_in.1, s32[31,128]{1,0:T(8,128)} %order_in.1), custom_call_target="tpu_custom_call" | custom-call | tf_op jit(solution)/shard_map/pallas_call | solution.py:337
  30.0 1.5 %shard_map.69 = (bf16[4096,128]{1,0:T(8,128)(2,1)}, f32[31,64,64]{2,1,0:T(8,128)}) custom-call(bf16[4096,128]{1,0:T(8,128)(2,1)S(1)} %get-tuple-element.7.flux_in, bf16[8,2,64,128]{3,2,1,0:T(8,128)(2,1)S(1)} %get-tuple-element.8.g2, bf16[15,64,128]{2,1,0:T(8,128)(2,1)S(1)} %get-tuple-element.9.hots), custom_call_target="tpu_custom_call" | custom-call | tf_op jit(solution)/shard_map/pallas_call | solution.py:390

commit v4 on v3

--- a/solution.py
+++ b/solution.py
@@ -59,8 +59,8 @@
     ngx, ngy, k_count, planes, cx, cy,
     states_in, classes_in, perm_in, cands_in, order_in, flux_out, g2, hots,
     states, classes, perm, cands, order, rowst, insem,
-    st32, flux32, ksc, tx, ty, tz, xs, xr, kxs, kxr, ys, yr, ky, kyr, yface, ordt, onehot, g1,
-    xsend, xrecv, ysend, yrecv, g1send, g1recv, g2send, g2recv, sibsend, sibrecv,
+    st32, flux32, ksc, tx, ty, tz, xs, xr, kxs, kxr, ys, yr, ky, kyr, yface, ke, cs, cr, ordt, onehot, g1,
+    csend, crecv, xsend, xrecv, ysend, yrecv, g1send, g1recv, g2send, g2recv, sibsend, sibrecv,
 ):
     a = lax.axis_index("gx")
     b = lax.axis_index("gy")
@@ -111,6 +111,9 @@
         return remote(
             kxs.at[side], kxr.at[1 - side], xsend.at[side, CHUNKS], xrecv.at[1 - side, CHUNKS], x_dev[side]
         )
+
+    def c_copy(side):
+        return remote(cs.at[side], cr.at[1 - side], csend.at[side], crecv.at[1 - side], x_dev[side])
 
     def y_copy(side):
         return remote(ys, yr.at[1 - side], ysend.at[side], yrecv.at[1 - side], y_dev[side])
@@ -141,6 +144,31 @@
     for c in range(1, CHUNKS):
         load(c).wait()
         widen(c)
+    small[2].wait()
+    lane_k = lax.broadcasted_iota(jnp.int32, (k_count, cy), 1)
+
+    def at_cell(ref, row, col):
+        found = ref[pl.ds(row, k_count, stride=zx), :]
+        return jnp.sum(jnp.where(lane_k == col, found, 0.0), axis=1, keepdims=True)
+
+    blank = jnp.zeros((k_count, cy), F32)
+    for side, x in ((0, 0), (1, cx - 1)):
+        def lend(i4, acc, side=side, x=x):
+            p_acc, s_acc = acc
+            for u in range(4):
+                i = i4 * 4 + u
+                cell = cands[x_dev[side][0], b, i]
+                plane = lax.div(cell, cx * cy)
+                col = lax.rem(cell, cy)
+                p_acc = jnp.where(lane_k == i, at_cell(st32.at[0], plane * cx + x, col), p_acc)
+                s_acc = jnp.where(lane_k == i, at_cell(st32.at[1], plane * cx + x, col), s_acc)
+            return p_acc, s_acc
+
+        lent_p, lent_s = lax.fori_loop(0, k_count // 4, lend, (blank, blank))
+        cs[side, 0:k_count, :] = lent_p.astype(BF16)
+        cs[side, k_count : 2 * k_count, :] = lent_s.astype(BF16)
+        c_copy(side).start()
+    for c in range(1, CHUNKS):
         for side in range(2):
             x_copy(side, c).start()
 
@@ -180,24 +208,7 @@
     ty[...] = jnp.where(lane == cy - 1, 0.0, transmit(k3, pltpu.roll(k3, cy - 1, axis=2)))
     tz[...] = transmit(k3[:-1], k3[1:])
 
-    def inner(s, carry):
-        at = pl.ds(pl.multiple_of(s * zx, zx), zx)
-        p = st32[0, at, :].reshape(cube)
-        sat = st32[1, at, :].reshape(cube)
-        m = sat * sat
-        fx = tx[...] * (m + pltpu.roll(m, cx - 1, axis=1)) * (pltpu.roll(p, cx - 1, axis=1) - p)
-        fy = ty[...] * (m + pltpu.roll(m, cy - 1, axis=2)) * (pltpu.roll(p, cy - 1, axis=2) - p)
-        fz = tz[...] * (m[:-1] + m[1:]) * (p[1:] - p[:-1])
-        total = (fx - pltpu.roll(fx, 1, axis=1)) + (fy - pltpu.roll(fy, 1, axis=2))
-        zero = jnp.zeros((1, cx, cy), F32)
-        total = total + (jnp.concatenate([fz, zero], axis=0) - jnp.concatenate([zero, fz], axis=0))
-        flux32[at, :] = total.reshape(zx, cy)
-        return carry
-
-    lax.fori_loop(0, k_count, inner, 0, unroll=2)
-
     small[3].wait()
-    small[2].wait()
     ordt[...] = jnp.zeros(ordt.shape, F32)
     ordt[0:nodes, :] = order[...].astype(F32)
     turned = ordt[...].T
@@ -223,54 +234,65 @@
         p1, s_1 = across(low[:cx], high[:cx]), across(low[cx:], high[cx:])
         yface[t] = kcol * (own[cx:] * own[cx:] + s_1 * s_1) * (p1 - own[:cx])
 
+    rim = (lane1 == 0) | (lane1 == cy - 1)
+    in_block = cy // 2 // planes
+
+    def inner(t, carry):
+        for u in range(in_block):
+            at = pl.ds(pl.multiple_of(t * block, block) + u * zx, zx)
+            p = st32[0, at, :].reshape(cube)
+            sat = st32[1, at, :].reshape(cube)
+            m = sat * sat
+            fx = tx[...] * (m + pltpu.roll(m, cx - 1, axis=1)) * (pltpu.roll(p, cx - 1, axis=1) - p)
+            fy = ty[...] * (m + pltpu.roll(m, cy - 1, axis=2)) * (pltpu.roll(p, cy - 1, axis=2) - p)
+            fz = tz[...] * (m[:-1] + m[1:]) * (p[1:] - p[:-1])
+            total = (fx - pltpu.roll(fx, 1, axis=1)) + (fy - pltpu.roll(fy, 1, axis=2))
+            zero = jnp.zeros((1, cx, cy), F32)
+            total = total + (jnp.concatenate([fz, zero], axis=0) - jnp.concatenate([zero, fz], axis=0))
+            face = yface[t]
+            fix = []
+            for v in range(planes):
+                fix.append(jnp.where(rim, pltpu.roll(face, cy - 1 - 2 * (u * planes + v), axis=1), 0.0))
+            flux32[at, :] = total.reshape(zx, cy) + jnp.concatenate(fix, axis=0)
+        return carry
+
+    lax.fori_loop(0, blocks, inner, 0)
+
     for side in range(2):
-        kx_copy(side).wait_recv()
-    kedge = [transmit(kxs[side], kxr[side]) for side in range(2)]
-    kedge = [jnp.concatenate([one, one], axis=0) for one in kedge]
-    rim = (lane1 == 0) | (lane1 == cy - 1)
-    lane_k = lax.broadcasted_iota(jnp.int32, (per, cy), 1)
-    for c in range(CHUNKS):
-        for side in range(2):
-            x_copy(side, c).wait_recv()
-
-        for j in range(c * per // 8, (c + 1) * per // 8):
-            def outer(i, carry, j=j, c=c):
-                s0 = j * 8 + 2 * i
-                local = s0 - c * per
-                at = pl.ds(s0 * zx, 2 * zx)
-                for side, x in ((0, 0), (1, cx - 1)):
-                    rp = pl.ds(local * planes, 2 * planes)
-                    rs = pl.ds((per + local) * planes, 2 * planes)
-                    p0, s_0 = xs[side, c, rp, :].astype(F32), xs[side, c, rs, :].astype(F32)
-                    p1, s_1 = xr[side, c, rp, :].astype(F32), xr[side, c, rs, :].astype(F32)
-                    face = kedge[side] * (s_0 * s_0 + s_1 * s_1) * (p1 - p0)
-                    rows = pl.ds(s0 * zx + x, 2 * planes, stride=cx)
-                    flux32[rows, :] = flux32[rows, :] + face
-                fix = []
-                for v in range(2 * planes):
-                    t, u = divmod(s0 * planes + v, cy // 2)
-                    fix.append(jnp.where(rim, pltpu.roll(yface[t], cy - 1 - 2 * u, axis=1), 0.0))
-                total = flux32[at, :] + jnp.concatenate(fix, axis=0)
-                flux32[at, :] = total
-                flux_out[at, :] = total.astype(BF16)
-                return carry
-
-            for i in range(4):
-                outer(i, 0)
-
-        def take(i16, acc, c=c):
-            for u in range(16):
-                i = i16 * 16 + u
-                cell = cands[a, b, i]
-                row = lax.div(cell, cy)
-                found = flux32[pl.ds(c * per * zx + row, per, stride=zx), :]
-                value = jnp.sum(jnp.where(lane_k == cell - row * cy, found, 0.0), axis=1, keepdims=True)
-                acc = jnp.where(lane_k == i, value, acc)
-            return acc
-
-        rowst[c * per : (c + 1) * per, :] = lax.fori_loop(0, k_count // 16, take, jnp.zeros((per, cy), F32))
-
-    picked = rowst[...].T[:k_count]
+        kx_copy(1 - side).wait_recv()
+        ke[side] = transmit(kxs[side], kxr[side])
+    lane_1 = lax.broadcasted_iota(jnp.int32, (1, cy), 1)
+
+    def take(i4, acc):
+        f_acc, p_acc, s_acc, low_acc, high_acc = acc
+        for u in range(4):
+            i = i4 * 4 + u
+            cell = cands[a, b, i]
+            row = lax.div(cell, cy)
+            col = cell - row * cy
+            plane = lax.div(row, cx)
+            x = row - plane * cx
+            f_acc = jnp.where(lane_k == i, at_cell(flux32, row, col), f_acc)
+            p_acc = jnp.where(lane_k == i, at_cell(st32.at[0], row, col), p_acc)
+            s_acc = jnp.where(lane_k == i, at_cell(st32.at[1], row, col), s_acc)
+            edge = []
+            for side, at_x in ((0, 0), (1, cx - 1)):
+                line = ke[side, pl.ds(plane, 1), :]
+                value = jnp.sum(jnp.where(lane_1 == col, line, 0.0), axis=1, keepdims=True)
+                edge.append(value * (x == at_x).astype(F32))
+            low_acc = jnp.where(lane_1 == i, edge[0], low_acc)
+            high_acc = jnp.where(lane_1 == i, edge[1], high_acc)
+        return f_acc, p_acc, s_acc, low_acc, high_acc
+
+    thin = jnp.zeros((1, cy), F32)
+    f_acc, p_acc, s_acc, low_acc, high_acc = lax.fori_loop(
+        0, k_count // 4, take, (blank, blank, blank, thin, thin)
+    )
+    for side, t_acc in ((0, low_acc), (1, high_acc)):
+        c_copy(1 - side).wait_recv()
+        p1, s_1 = cr[side, 0:k_count, :].astype(F32), cr[side, k_count : 2 * k_count, :].astype(F32)
+        f_acc = f_acc + t_acc * (s_acc * s_acc + s_1 * s_1) * (p1 - p_acc)
+    picked = f_acc.T[:k_count]
     high = picked.astype(BF16).astype(F32)
     mine = jnp.concatenate([high, picked - high], axis=1).astype(BF16)
     g1[b] = mine
@@ -280,6 +302,26 @@
 
     for d in range(1, ngy):
         g1_copy(d, b, (a, lax.rem(b + d, ngy))).start()
+
+    kedge = [jnp.concatenate([ke[side], ke[side]], axis=0) for side in range(2)]
+
+    def outer(c):
+        for side in range(2):
+            x_copy(side, c).wait_recv()
+        for local in range(0, per, 2):
+            s0 = c * per + local
+            at = pl.ds(s0 * zx, 2 * zx)
+            rp = pl.ds(local * planes, 2 * planes)
+            rs = pl.ds((per + local) * planes, 2 * planes)
+            for side, x in ((0, 0), (1, cx - 1)):
+                p0, s_0 = xs[side, c, rp, :].astype(F32), xs[side, c, rs, :].astype(F32)
+                p1, s_1 = xr[side, c, rp, :].astype(F32), xr[side, c, rs, :].astype(F32)
+                face = kedge[side] * (s_0 * s_0 + s_1 * s_1) * (p1 - p0)
+                rows = pl.ds(s0 * zx + x, 2 * planes, stride=cx)
+                flux32[rows, :] = flux32[rows, :] + face
+            flux_out[at, :] = flux32[at, :].astype(BF16)
+
+    outer(0)
     for d in range(1, ngy):
         g1_copy(d, lax.rem(b + ngy - d, ngy), (a, lax.rem(b + d, ngy))).wait_recv()
 
@@ -300,15 +342,19 @@
 
     for d in range(1, ngx):
         g2_copy(d, a, (lax.rem(a + d, ngx), b)).start()
+    for c in range(1, CHUNKS - 1):
+        outer(c)
     for d in range(1, ngx):
         slot = lax.rem(a + ngx - d, ngx)
         g2_copy(d, slot, (lax.rem(a + d, ngx), b)).wait_recv()
         sib_copy(d, slot, own).start()
+    outer(CHUNKS - 1)
     for d in range(1, ngx):
         sib_copy(d, lax.rem(a + ngx - d, ngx), other).wait_recv()
 
     for side in range(2):
         kx_copy(side).wait_send()
+        c_copy(side).wait_send()
         y_copy(side).wait_send()
         ky_copy(side).wait_send()
         for c in range(CHUNKS):
@@ -366,9 +412,14 @@
                 pltpu.VMEM((cx, cy), F32),
                 pltpu.VMEM((2, cx, cy), F32),
                 pltpu.VMEM((blocks, cx, cy), F32),
+                pltpu.VMEM((2, planes, cy), F32),
+                pltpu.VMEM((2, 2 * k, cy), BF16),
+                pltpu.VMEM((2, 2 * k, cy), BF16),
                 pltpu.VMEM((padded, 2 * k), F32),
                 pltpu.VMEM((tiles // 2, k, 2 * k), BF16),
                 pltpu.VMEM((ngy, k, 2 * k), BF16),
+                dma((2,)),
+                dma((2,)),
                 dma((2, CHUNKS + 1)),
                 dma((2, CHUNKS + 1)),
                 dma((4,)),

time: 31.6 us -> 45.3 us (1.43)
  Pallas kernels: 30.8 us -> 44.5 us
    pallas_call x1, Pallas kernels: 29.3 us -> 43.1 us  [local(): pl.pallas_call(functools.partial(kernel, ngx, ngy, k, planes, cx, cy), ou...]
where the time goes in v4:
time: 45.3 us; the launch traced here: 45.2 us
  Pallas kernels  44.5 us (98%)
  between operations  0.64 us (1%)
    pallas_call x1, Pallas kernels, local(): pl.pallas_call(functools.partial(kernel, ngx, ngy, k, planes, cx, cy), ou...  43.1 us
    pallas_call x1, Pallas kernels, local(): pl.pallas_call(functools.partial(finish, k), out_shape=(jax.ShapeDtypeStr...  1.46 us

profile of v4, /device:TPU:0, one launch (start us, length us, event | category | flops | bytes accessed | tf_op | source)
XLA Modules:
  0.0 45.2 jit_solution(7842582450297269155)
XLA Ops:
  0.6 43.1 %shard_map.68 = (bf16[4096,128]{1,0:T(8,128)(2,1)S(1)}, bf16[8,2,64,128]{3,2,1,0:T(8,128)(2,1)S(1)}, bf16[15,64,128]{2,1,0:T(8,128)(2,1)S(1)}) custom-call(bf16[2,4096,128]{2,1,0:T(8,128)(2,1)} %bitcast.3, s32[64,128]{1,0:T(8,128)} %bitcast.4, f32[8]{0:T(128)} %perm_in.1, s32[8,4,64]{2,1,0:T(4,128)} %cands_in.1, s32[31,128]{1,0:T(8,128)} %order_in.1), custom_call_target="tpu_custom_call" | custom-call | tf_op jit(solution)/shard_map/pallas_call | solution.py:383
  43.7 1.5 %shard_map.69 = (bf16[4096,128]{1,0:T(8,128)(2,1)}, f32[31,64,64]{2,1,0:T(8,128)}) custom-call(bf16[4096,128]{1,0:T(8,128)(2,1)S(1)} %get-tuple-element.7.flux_in, bf16[8,2,64,128]{3,2,1,0:T(8,128)(2,1)S(1)} %get-tuple-element.8.g2, bf16[15,64,128]{2,1,0:T(8,128)(2,1)S(1)} %get-tuple-element.9.hots), custom_call_target="tpu_custom_call" | custom-call | tf_op jit(solution)/shard_map/pallas_call | solution.py:441

commit v5 on v4

--- a/solution.py
+++ b/solution.py
@@ -147,9 +147,8 @@
     small[2].wait()
     lane_k = lax.broadcasted_iota(jnp.int32, (k_count, cy), 1)
 
-    def at_cell(ref, row, col):
-        found = ref[pl.ds(row, k_count, stride=zx), :]
-        return jnp.sum(jnp.where(lane_k == col, found, 0.0), axis=1, keepdims=True)
+    def at_cell(ref, row, turn):
+        return pltpu.roll(ref[pl.ds(row, k_count, stride=zx), :], turn, axis=1)
 
     blank = jnp.zeros((k_count, cy), F32)
     for side, x in ((0, 0), (1, cx - 1)):
@@ -159,9 +158,9 @@
                 i = i4 * 4 + u
                 cell = cands[x_dev[side][0], b, i]
                 plane = lax.div(cell, cx * cy)
-                col = lax.rem(cell, cy)
-                p_acc = jnp.where(lane_k == i, at_cell(st32.at[0], plane * cx + x, col), p_acc)
-                s_acc = jnp.where(lane_k == i, at_cell(st32.at[1], plane * cx + x, col), s_acc)
+                turn = lax.rem(i + cy - lax.rem(cell, cy), cy)
+                p_acc = jnp.where(lane_k == i, at_cell(st32.at[0], plane * cx + x, turn), p_acc)
+                s_acc = jnp.where(lane_k == i, at_cell(st32.at[1], plane * cx + x, turn), s_acc)
             return p_acc, s_acc
 
         lent_p, lent_s = lax.fori_loop(0, k_count // 4, lend, (blank, blank))
@@ -269,17 +268,16 @@
             i = i4 * 4 + u
             cell = cands[a, b, i]
             row = lax.div(cell, cy)
-            col = cell - row * cy
+            turn = lax.rem(i + cy - (cell - row * cy), cy)
             plane = lax.div(row, cx)
             x = row - plane * cx
-            f_acc = jnp.where(lane_k == i, at_cell(flux32, row, col), f_acc)
-            p_acc = jnp.where(lane_k == i, at_cell(st32.at[0], row, col), p_acc)
-            s_acc = jnp.where(lane_k == i, at_cell(st32.at[1], row, col), s_acc)
+            f_acc = jnp.where(lane_k == i, at_cell(flux32, row, turn), f_acc)
+            p_acc = jnp.where(lane_k == i, at_cell(st32.at[0], row, turn), p_acc)
+            s_acc = jnp.where(lane_k == i, at_cell(st32.at[1], row, turn), s_acc)
             edge = []
             for side, at_x in ((0, 0), (1, cx - 1)):
-                line = ke[side, pl.ds(plane, 1), :]
-                value = jnp.sum(jnp.where(lane_1 == col, line, 0.0), axis=1, keepdims=True)
-                edge.append(value * (x == at_x).astype(F32))
+                line = pltpu.roll(ke[side, pl.ds(plane, 1), :], turn, axis=1)
+                edge.append(line * (x == at_x).astype(F32))
             low_acc = jnp.where(lane_1 == i, edge[0], low_acc)
             high_acc = jnp.where(lane_1 == i, edge[1], high_acc)
         return f_acc, p_acc, s_acc, low_acc, high_acc

time: 45.3 us -> 44.9 us (level)
  no operation moved by 1% of the time
where the time goes in v5:
time: 44.9 us; the launch traced here: 44.7 us
  Pallas kernels  44.1 us (98%)
  between operations  0.64 us (1%)
    pallas_call x1, Pallas kernels, local(): pl.pallas_call(functools.partial(kernel, ngx, ngy, k, planes, cx, cy), ou...  42.6 us
    pallas_call x1, Pallas kernels, local(): pl.pallas_call(functools.partial(finish, k), out_shape=(jax.ShapeDtypeStr...  1.46 us

profile of v5, /device:TPU:0, one launch (start us, length us, event | category | flops | bytes accessed | tf_op | source)
XLA Modules:
  0.0 44.7 jit_solution(3593548652733313486)
XLA Ops:
  0.6 42.6 %shard_map.68 = (bf16[4096,128]{1,0:T(8,128)(2,1)S(1)}, bf16[8,2,64,128]{3,2,1,0:T(8,128)(2,1)S(1)}, bf16[15,64,128]{2,1,0:T(8,128)(2,1)S(1)}) custom-call(bf16[2,4096,128]{2,1,0:T(8,128)(2,1)} %bitcast.3, s32[64,128]{1,0:T(8,128)} %bitcast.4, f32[8]{0:T(128)} %perm_in.1, s32[8,4,64]{2,1,0:T(4,128)} %cands_in.1, s32[31,128]{1,0:T(8,128)} %order_in.1), custom_call_target="tpu_custom_call" | custom-call | tf_op jit(solution)/shard_map/pallas_call | solution.py:381
  43.3 1.5 %shard_map.69 = (bf16[4096,128]{1,0:T(8,128)(2,1)}, f32[31,64,64]{2,1,0:T(8,128)}) custom-call(bf16[4096,128]{1,0:T(8,128)(2,1)S(1)} %get-tuple-element.7.flux_in, bf16[8,2,64,128]{3,2,1,0:T(8,128)(2,1)S(1)} %get-tuple-element.8.g2, bf16[15,64,128]{2,1,0:T(8,128)(2,1)S(1)} %get-tuple-element.9.hots), custom_call_target="tpu_custom_call" | custom-call | tf_op jit(solution)/shard_map/pallas_call | solution.py:439

commit v6 on v3

--- a/solution.py
+++ b/solution.py
@@ -10,7 +10,7 @@
 MESH = pl.DeviceIdType.MESH
 F32 = jnp.float32
 BF16 = jnp.bfloat16
-CHUNKS = 4
+CHUNKS = 8
 
 
 def remote(src, dst, send, recv, device):
@@ -264,7 +264,7 @@
                 cell = cands[a, b, i]
                 row = lax.div(cell, cy)
                 found = flux32[pl.ds(c * per * zx + row, per, stride=zx), :]
-                value = jnp.sum(jnp.where(lane_k == cell - row * cy, found, 0.0), axis=1, keepdims=True)
+                value = pltpu.roll(found, lax.rem(i + cy - (cell - row * cy), cy), axis=1)
                 acc = jnp.where(lane_k == i, value, acc)
             return acc
 

time: 31.6 us -> 32.4 us (1.025)
  Pallas kernels: 30.8 us -> 31.6 us
    pallas_call x1, Pallas kernels: 29.3 us -> 30.1 us  [local(): pl.pallas_call(functools.partial(kernel, ngx, ngy, k, planes, cx, cy), ou...]
where the time goes in v6:
time: 32.4 us; the launch traced here: 32.2 us
  Pallas kernels  31.6 us (98%)
  between operations  0.64 us (2%)
    pallas_call x1, Pallas kernels, local(): pl.pallas_call(functools.partial(kernel, ngx, ngy, k, planes, cx, cy), ou...  30.1 us
    pallas_call x1, Pallas kernels, local(): pl.pallas_call(functools.partial(finish, k), out_shape=(jax.ShapeDtypeStr...  1.46 us

profile of v6, /device:TPU:0, one launch (start us, length us, event | category | flops | bytes accessed | tf_op | source)
XLA Modules:
  0.0 32.2 jit_solution(11640785801361235601)
XLA Ops:
  0.6 30.1 %shard_map.68 = (bf16[4096,128]{1,0:T(8,128)(2,1)S(1)}, bf16[8,2,64,128]{3,2,1,0:T(8,128)(2,1)S(1)}, bf16[15,64,128]{2,1,0:T(8,128)(2,1)S(1)}) custom-call(bf16[2,4096,128]{2,1,0:T(8,128)(2,1)} %bitcast.3, s32[64,128]{1,0:T(8,128)} %bitcast.4, f32[8]{0:T(128)} %perm_in.1, s32[8,4,64]{2,1,0:T(4,128)} %cands_in.1, s32[31,128]{1,0:T(8,128)} %order_in.1), custom_call_target="tpu_custom_call" | custom-call | tf_op jit(solution)/shard_map/pallas_call | solution.py:337
  30.7 1.5 %shard_map.69 = (bf16[4096,128]{1,0:T(8,128)(2,1)}, f32[31,64,64]{2,1,0:T(8,128)}) custom-call(bf16[4096,128]{1,0:T(8,128)(2,1)S(1)} %get-tuple-element.7.flux_in, bf16[8,2,64,128]{3,2,1,0:T(8,128)(2,1)S(1)} %get-tuple-element.8.g2, bf16[15,64,128]{2,1,0:T(8,128)(2,1)S(1)} %get-tuple-element.9.hots), custom_call_target="tpu_custom_call" | custom-call | tf_op jit(solution)/shard_map/pallas_call | solution.py:390
